TPU v7x, 32 devices: a whole 2x2x4 slice. The times are simulated.
32 devices in a mesh: groups: 2 (over y), node: 4 (over z), feat: 4 (over x, core).
Axes of the slice: x: 2, y: 2, z: 4, core: 2. Of those that a mesh axis runs over, the one named last changes fastest.
Arguments:
- features: bfloat16 [12288, 256], P(('groups', 'node'), 'feat'), parts along dimension 0, may hold values from -6 to 6
- tiles: bfloat16 [96, 8, 128, 128], P(('groups', 'node')), parts along dimension 0, may hold values from 0 to 0.0625
- col_block: int32 [96, 8], P(('groups', 'node')), parts along dimension 0, may hold values from 0 to 47, as said below
- weight: bfloat16 [256, 172], replicated, may hold values from -0.375 to 0.375
- bias: float32 [172], replicated, may hold values from -1 to 1
Outputs:
- logits: bfloat16 [12288, 172], P(('groups', 'node', 'feat')), parts along dimension 0
There are 2 independent parts, one for each index of `groups`. A program takes and returns all parts, laid end to end along the dimension named above; an argument that names none is the same for every part. Nothing has to cross between parts.
Inputs may be any that keep to these rules, and one draw needn't show every extreme that they name: `col_block`: stripe d holds block rows d * 12 to (d + 1) * 12 - 1. Slot 0 of block row r is r itself; every other slot names a block of another stripe. Over the block rows of one stripe, at most 28 slots name blocks of any one other stripe, and exactly 28 name blocks of some other stripe. The same block may be named more than once.
All inputs are finite; a program needn't handle non-finite values.
Results may differ from a plain program's by a relative error of at most 0.0046.
Values may be sent and summed in bfloat16 or wider, within the bound.
No kernel may reach another device: no remote copies, remote signals or barrier semaphores. Data moves between devices by JAX's collectives and lax.ppermute only.
A program may use at most 128 MiB of HBM per device.

v0:
```python
import jax
import jax.numpy as jnp
from jax import lax
from jax.sharding import PartitionSpec as P


def on_device(features, tiles, col_block, weight, bias):
    stripe_blocks, slot_count, block_size, _ = tiles.shape
    feat_width = features.shape[1]
    own_blocks = features.reshape(stripe_blocks, block_size, feat_width)
    remote_cols = col_block[:, 1:].reshape(-1)
    gathered = lax.all_gather(features, "node", axis=0, tiled=True)
    all_blocks = gathered.reshape(-1, block_size, feat_width)
    fetched = all_blocks[remote_cols]
    fetched = fetched.reshape(stripe_blocks, slot_count - 1, block_size, feat_width)
    local_sum = jnp.einsum(
        "rij,rjf->rif", tiles[:, 0], own_blocks, preferred_element_type=jnp.float32
    )
    remote_sum = jnp.einsum(
        "rkij,rkjf->rif", tiles[:, 1:], fetched, preferred_element_type=jnp.float32
    )
    aggregated = (local_sum + remote_sum).astype(jnp.bfloat16).reshape(-1, feat_width)
    rows_full = lax.all_to_all(aggregated, "feat", split_axis=0, concat_axis=1, tiled=True)
    logits = jnp.dot(rows_full, weight, preferred_element_type=jnp.float32)
    return (logits + bias).astype(jnp.bfloat16)


def solution(mesh):
    in_specs = (
        P(("groups", "node"), "feat"),
        P(("groups", "node"), None, None, None),
        P(("groups", "node"), None),
        P(),
        P(),
    )
    out_specs = P(("groups", "node", "feat"), None)
    return jax.shard_map(
        on_device, mesh=mesh, in_specs=in_specs, out_specs=out_specs, check_vma=False
    )
```

profile of v0, /device:TPU:0, one launch (start us, length us, event | category | flops | bytes accessed | tf_op | source)
XLA Modules:
  0.0 37.0 jit_solution(2078628646601903065)
XLA Ops:
  0.0 0.0 copy-start
  0.0 0.7 %slice.10 = s32[12,7]{0,1:T(8,128)S(1)} slice(s32[12,8]{0,1:T(8,128)} %param.7), slice={[0:12], [1:8]} | slice | bytes 672 | tf_op jit(solution)/shard_map/slice | solution.py:11
  0.7 0.1 copy.23
  0.8 0.1 reshape.48
  0.9 21.5 %all_gather.3 = bf16[6144,64]{0,1:T(8,128)(2,1)S(1)} all-gather(bf16[1536,64]{0,1:T(8,128)(2,1)} %param.5), channel_id=1, replica_groups=mesh['groups'=2,'node'=4,'feat'=4] {'node'}, dimensions={0}, use_global_device_ids=true | all-gather | bytes 983040 | tf_op jit(solution)/shard_map/all_gather | solution.py:12
  22.4 0.2 copy_bitcast_fusion
  22.7 0.8 %gather_fusion = bf16[84,128,64]{1,2,0:T(8,128)(2,1)S(1)} fusion(bf16[48,128,64]{1,2,0:T(8,128)(2,1)S(1)} %copy_bitcast_fusion, s32[1024]{0:T(1024)S(1)} %pad_clamp_fusion), kind=kCustom, calls=%fused_computation | custom fusion | bytes 2752848 | tf_op jit(solution)/shard_map/gather | solution.py:14
  23.5 0.0 copy-start.1
  23.5 0.0 copy-start.2
  23.5 3.0 %fusion.2 = f32[12,128,64]{1,2,0:T(8,128)S(1)} fusion(bf16[12,7,128,64]{2,3,1,0:T(8,128)(2,1)S(1)} %bitcast.33, bf16[12,8,128,128]{3,2,1,0:T(8,128)(2,1)} %param.6), kind=kOutput, calls=%fused_computation.3 | convolution fusion | flops 176160768 | bytes 4521984 | tf_op jit(solution)/shard_map/rkij,rkjf->rif/dot_general | solution.py:19
  26.5 0.0 copy-done.1
  26.5 1.4 %fusion.5 = bf16[12,128,64]{1,2,0:T(8,128)(2,1)S(1)} fusion(f32[12,128,64]{1,2,0:T(8,128)S(1)} %fusion.2, bf16[12,8,128,128]{3,2,1,0:T(8,128)(2,1)} %param.6, bf16[1536,64]{0,1:T(8,128)(2,1)S(1)} %copy-done.1), kind=kOutput, calls=%fused_computation.5 | convolution fusion | flops 25362432 | bytes 1179648 | tf_op jit(solution)/shard_map/rij,rjf->rif/dot_general | solution.py:16
  27.9 0.1 copy.25
  28.0 0.1 all_to_all.14
  28.2 7.9 %all_to_all.19 = bf16[4,384,64]{1,2,0:T(8,128)(2,1)S(1)} all-to-all(bf16[4,384,64]{1,2,0:T(8,128)(2,1)S(1)} %copy.26), channel_id=1, replica_groups=mesh['groups'=2,'node'=4,'feat'=4] {'feat'}, dimensions={0} | all-to-all | bytes 393216 | tf_op jit(solution)/shard_map/all_to_all | solution.py:23
  36.1 0.0 copy-done
  36.1 0.0 copy-done.2
  36.1 0.9 %fusion.6 = bf16[384,172]{0,1:T(8,128)(2,1)} fusion(bf16[384,256]{0,1:T(8,128)(2,1)S(1)} %bitcast.34, bf16[256,172]{0,1:T(8,128)(2,1)S(1)} %copy-done, f32[172]{0:T(256)S(1)} %copy-done.2), kind=kOutput, calls=%fused_computation.7 | convolution fusion | flops 33948672 | bytes 417456 | tf_op jit(solution)/shard_map/dot_general | solution.py:24
  (3 shorter events, 0.0 us)
Async XLA Ops:
  0.0 36.1 %copy-start = (bf16[256,172]{0,1:T(8,128)(2,1)S(1)}, bf16[256,172]{0,1:T(8,128)(2,1)}, u32[]{:S(2)}) copy-start(bf16[256,172]{0,1:T(8,128)(2,1)} %param.8) | copy-start | bytes 264196
  23.5 3.0 %copy-start.1 = (bf16[1536,64]{0,1:T(8,128)(2,1)S(1)}, bf16[1536,64]{0,1:T(8,128)(2,1)}, u32[]{:S(2)}) copy-start(bf16[1536,64]{0,1:T(8,128)(2,1)} %param.5) | copy-start | bytes 589828
  23.5 12.6 %copy-start.2 = (f32[172]{0:T(256)S(1)}, f32[172]{0:T(256)}, u32[]{:S(2)}) copy-start(f32[172]{0:T(256)} %param.9) | copy-start | bytes 2068
where the time goes:
time: 37.2 us; the launch traced here: 37 us
  blocking collectives  29.4 us (79%)
  matrix products  5.22 us (14%)
  local copies, waits for them, and re-layouts  2.25 us (6%)
    all_gather x1, blocking collectives, on_device(): gathered = lax.all_gather(features, 'node', axis=0, tiled=True)  21.5 us
    all_to_all x1, blocking collectives, on_device(): lax.all_to_all(aggregated, 'feat', split_axis=0, concat_axis=1, tiled=True)  7.89 us
    dot_general x1, matrix products, on_device(): jnp.einsum('rkij,rkjf->rif', tiles[:, 1:], fetched, preferred_element_typ...  2.98 us
    dot_general x1, matrix products, on_device(): jnp.einsum('rij,rjf->rif', tiles[:, 0], own_blocks, preferred_element_typ...  1.37 us
    dot_general x1, matrix products, on_device(): logits = jnp.dot(rows_full, weight, preferred_element_type=jnp.float32)  0.87 us
    slice x2, local copies, waits for them, and re-layouts, on_device(): remote_cols = col_block[:, 1:].reshape(-1)  0.82 us
    gather x1, local copies, waits for them, and re-layouts, on_device(): fetched = all_blocks[remote_cols]  0.81 us

commit v1 on v0

v1 whole, which is shorter than its diff:
```python
import functools

import jax
import jax.numpy as jnp
from jax import lax
from jax.experimental import pallas as pl
from jax.experimental.pallas import tpu as pltpu
from jax.sharding import PartitionSpec as P

VMEM = pl.BlockSpec(memory_space=pltpu.VMEM)
SMEM = pl.BlockSpec(memory_space=pltpu.SMEM)


def times_tile(block_t, tile):
    return lax.dot_general(
        block_t, tile, (((1,), (1,)), ((), ())), preferred_element_type=jnp.float32
    )


def own_kernel(me_ref, col_ref, x_ref, tiles_ref, acc_ref, list_ref, count):
    slot_count, stripe_blocks = col_ref.shape
    size = tiles_ref.shape[-1]
    sources, _ = list_ref.shape
    for source in range(sources):
        count[source] = 0
    for row in range(stripe_blocks):
        for slot in range(1, slot_count):
            column = col_ref[slot, row]
            stripe = lax.div(column, stripe_blocks)
            which = (stripe ^ me_ref[0]) - 1
            at = count[which]
            list_ref[which, at] = (row * slot_count + slot) * stripe_blocks + (
                column - stripe * stripe_blocks
            )
            count[which] = at + 1
    for row in range(stripe_blocks):
        acc_ref[row] = times_tile(
            x_ref[:, row * size : (row + 1) * size], tiles_ref[row * slot_count]
        )


def add_slots(which, list_ref, x_ref, tiles_ref, acc_ref):
    stripe_blocks = acc_ref.shape[0]
    slot_count = tiles_ref.shape[0] // stripe_blocks
    size = tiles_ref.shape[-1]
    for entry in range(list_ref.shape[1]):
        code = list_ref[which, entry]
        slot = lax.div(code, stripe_blocks)
        column = code - slot * stripe_blocks
        block = x_ref[:, pl.ds(pl.multiple_of(column * size, size), size)]
        acc_ref[lax.div(slot, slot_count)] += times_tile(block, tiles_ref[slot])


def middle_kernel(list_ref, one_ref, two_ref, tiles_ref, acc_in, acc_ref):
    del acc_in
    add_slots(0, list_ref, one_ref, tiles_ref, acc_ref)
    add_slots(1, list_ref, two_ref, tiles_ref, acc_ref)


def last_kernel(feat_ref, list_ref, three_ref, tiles_ref, acc_in, acc_ref, *part_refs):
    del acc_in
    add_slots(2, list_ref, three_ref, tiles_ref, acc_ref)
    size = tiles_ref.shape[-1]
    share = acc_ref.shape[0] // len(part_refs)
    for k, part_ref in enumerate(part_refs):
        owner = feat_ref[0] ^ k
        for row in range(share):
            part_ref[:, row * size : (row + 1) * size] = acc_ref[
                owner * share + row
            ].astype(part_ref.dtype)


def project_kernel(feat_ref, weight_ref, bias_ref, *refs):
    part_refs, out_ref, rows = refs[:-2], refs[-2], refs[-1]
    width = part_refs[0].shape[0]
    for k, part_ref in enumerate(part_refs):
        owner = feat_ref[0] ^ k
        rows[pl.ds(pl.multiple_of(owner * width, width), width), :] = part_ref[...]
    total = jnp.dot(weight_ref[...], rows[...], preferred_element_type=jnp.float32)
    out_ref[...] = (total + bias_ref[...]).astype(out_ref.dtype)


def exchange(x, axis, size, bit):
    return lax.ppermute(x, axis, [(i, i ^ bit) for i in range(size)])


def on_line(stripes, slices, features, tiles, col_block, weight, bias):
    stripe_blocks, slot_count, size, _ = tiles.shape
    width = features.shape[1]
    remote = stripe_blocks * (slot_count - 1) // (stripes - 1)
    me = lax.axis_index("node").astype(jnp.int32).reshape(1)
    feat = lax.axis_index("feat").astype(jnp.int32).reshape(1)
    x = features.T
    two = exchange(x, "node", stripes, 2)
    one = exchange(x, "node", stripes, 1)
    three = exchange(two, "node", stripes, 1)

    params = pltpu.CompilerParams(vmem_limit_bytes=32 << 20)
    acc_shape = jax.ShapeDtypeStruct((stripe_blocks, width, size), jnp.float32)
    flat = tiles.reshape(-1, size, size)
    tile_flops = 2 * size * size * width
    acc, lists = pl.pallas_call(
        own_kernel,
        out_shape=(
            acc_shape,
            jax.ShapeDtypeStruct((stripes - 1, remote), jnp.int32),
        ),
        in_specs=[SMEM, SMEM, VMEM, VMEM],
        out_specs=(VMEM, SMEM),
        scratch_shapes=[pltpu.SMEM((stripes - 1,), jnp.int32)],
        compiler_params=params,
        cost_estimate=pl.CostEstimate(
            flops=stripe_blocks * tile_flops, bytes_accessed=flat.size * 4, transcendentals=0
        ),
        name="own",
    )(me, col_block.T, x, flat)
    acc = pl.pallas_call(
        middle_kernel,
        out_shape=acc_shape,
        in_specs=[SMEM, VMEM, VMEM, VMEM, VMEM],
        out_specs=VMEM,
        input_output_aliases={4: 0},
        compiler_params=params,
        cost_estimate=pl.CostEstimate(
            flops=2 * remote * tile_flops, bytes_accessed=flat.size * 4, transcendentals=0
        ),
        name="middle",
    )(lists, one, two, flat, acc)
    part_shape = jax.ShapeDtypeStruct((width, stripe_blocks // slices * size), jnp.bfloat16)
    _, *parts = pl.pallas_call(
        last_kernel,
        out_shape=(acc_shape,) + (part_shape,) * slices,
        in_specs=[SMEM, SMEM, VMEM, VMEM, VMEM],
        out_specs=(VMEM,) * (1 + slices),
        input_output_aliases={4: 0},
        compiler_params=params,
        cost_estimate=pl.CostEstimate(
            flops=remote * tile_flops, bytes_accessed=flat.size, transcendentals=0
        ),
        name="last",
    )(feat, lists, three, flat, acc)
    parts = parts[:1] + [exchange(parts[k], "feat", slices, k) for k in range(1, slices)]
    rows = part_shape.shape[1]
    classes = weight.shape[1]
    logits = pl.pallas_call(
        project_kernel,
        out_shape=jax.ShapeDtypeStruct((classes, rows), jnp.bfloat16),
        in_specs=[SMEM] + [VMEM] * (2 + slices),
        out_specs=VMEM,
        scratch_shapes=[pltpu.VMEM((slices * width, rows), jnp.bfloat16)],
        compiler_params=params,
        name="project",
    )(feat, weight.T, bias[:, None], *parts)
    return logits.T


def on_device(features, tiles, col_block, weight, bias):
    stripe_blocks, slot_count, size, _ = tiles.shape
    width = features.shape[1]
    gathered = lax.all_gather(features, "node", axis=0, tiled=True)
    fetched = gathered.reshape(-1, size, width)[col_block.reshape(-1)]
    fetched = fetched.reshape(stripe_blocks, slot_count, size, width)
    summed = jnp.einsum("rkij,rkjf->rif", tiles, fetched, preferred_element_type=jnp.float32)
    aggregated = summed.astype(jnp.bfloat16).reshape(-1, width)
    rows = lax.all_to_all(aggregated, "feat", split_axis=0, concat_axis=1, tiled=True)
    logits = jnp.dot(rows, weight, preferred_element_type=jnp.float32)
    return (logits + bias).astype(jnp.bfloat16)


def solution(mesh):
    stripes, slices = mesh.shape["node"], mesh.shape["feat"]
    line = stripes == 4 and slices & (slices - 1) == 0
    body = functools.partial(on_line, stripes, slices) if line else on_device
    in_specs = (
        P(("groups", "node"), "feat"),
        P(("groups", "node"), None, None, None),
        P(("groups", "node"), None),
        P(),
        P(),
    )
    out_specs = P(("groups", "node", "feat"), None)
    return jax.shard_map(
        body, mesh=mesh, in_specs=in_specs, out_specs=out_specs, check_vma=False
    )
```

time: 37.2 us -> 29.4 us (0.79)
  blocking collectives: 29.4 us -> 0 us
  waiting for transfers between devices: 0 us -> 11.1 us
  starting transfers between devices: 0 us -> 8.27 us
  Pallas kernels: 0 us -> 6.07 us
  matrix products: 5.22 us -> 0 us
  local copies, waits for them, and re-layouts: 2.25 us -> 3.63 us
    all_gather x1 -> x0, blocking collectives: 21.5 us -> none  [on_device(): gathered = lax.all_gather(features, 'node', axis=0, tiled=True)]
    ppermute x0 -> x6, waiting for transfers between devices: none -> 11.1 us  [exchange(): return lax.ppermute(x, axis, [(i, i ^ bit) for i in range(size)])]
    ppermute x0 -> x6, starting transfers between devices: none -> 8.27 us  [exchange(): return lax.ppermute(x, axis, [(i, i ^ bit) for i in range(size)])]
    all_to_all x1 -> x0, blocking collectives: 7.89 us -> none  [on_device(): lax.all_to_all(aggregated, 'feat', split_axis=0, concat_axis=1, tiled=True)]
    pallas_call x0 -> x4, Pallas kernels: none -> 6.07 us  [the longest x1 1.93 us: on_line(): pl.pallas_call(middle_kernel, out_shape=acc_shape, in_specs=[SMEM, VMEM,...]
    dot_general x3 -> x0, matrix products: 5.22 us -> none  [the longest x1 2.98 us: on_device(): jnp.einsum('rkij,rkjf->rif', tiles[:, 1:], fetched, preferred_element_typ...]
    unnamed x6 -> x12, local copies, waits for them, and re-layouts: 0.02 us -> 3.52 us
    slice x2 -> x0, local copies, waits for them, and re-layouts: 0.82 us -> none  [on_device(): remote_cols = col_block[:, 1:].reshape(-1)]
  transfers between devices with their start and end apart: 0 -> 6, of which waited for: 0 -> 3; matrix products, arithmetic and copies ran while one was open for 0% -> 0% of each run, Pallas kernels for 0% -> 13%
where the time goes in v1:
time: 29.4 us; the launch traced here: 29.2 us
  waiting for transfers between devices  11.1 us (38%)
  starting transfers between devices  8.27 us (28%)
  Pallas kernels  6.07 us (21%)
  local copies, waits for them, and re-layouts  3.63 us (12%)
    ppermute x6, waiting for transfers between devices, exchange(): return lax.ppermute(x, axis, [(i, i ^ bit) for i in range(size)])  11.1 us
    ppermute x6, starting transfers between devices, exchange(): return lax.ppermute(x, axis, [(i, i ^ bit) for i in range(size)])  8.27 us
    unnamed x12, local copies, waits for them, and re-layouts  3.52 us
    pallas_call x1, Pallas kernels, on_line(): pl.pallas_call(middle_kernel, out_shape=acc_shape, in_specs=[SMEM, VMEM,...  1.93 us
    pallas_call x1, Pallas kernels, on_line(): pl.pallas_call(own_kernel, out_shape=(acc_shape, jax.ShapeDtypeStruct((st...  1.91 us
    pallas_call x1, Pallas kernels, on_line(): pl.pallas_call(last_kernel, out_shape=(acc_shape,) + (part_shape,) * slic...  1.34 us
    pallas_call x1, Pallas kernels, on_line(): pl.pallas_call(project_kernel, out_shape=jax.ShapeDtypeStruct((classes, r...  0.88 us
  transfers between devices with their start and end apart: 6, of which 3 were waited for; matrix products, arithmetic and copies ran while one was open for 0% of the time, Pallas kernels for 13%

profile of v1, /device:TPU:0, one launch (start us, length us, event | category | flops | bytes accessed | tf_op | source)
XLA Modules:
  0.0 29.2 jit_solution(11235559335838583529)
XLA Ops:
  0.0 4.0 %collective-permute-start = (bf16[64,1536]{1,0:T(8,128)(2,1)}, bf16[64,1536]{1,0:T(8,128)(2,1)S(1)}, u32[]{:S(2)}, u32[]{:S(2)}) collective-permute-start(bf16[64,1536]{1,0:T(8,128)(2,1)} %bitcast.11), channel_id=1, source_target_pairs={{0,8},{4,12},{8,0},{12,4},{1,9},{5,13},{9,1},{13,5},{2,10},{6,14},... | collective-permute-start | bytes 589832 | tf_op jit(solution)/shard_map/ppermute | solution.py:84
  4.0 1.6 %collective-permute-start.2 = (bf16[64,1536]{1,0:T(8,128)(2,1)}, bf16[64,1536]{1,0:T(8,128)(2,1)S(1)}, u32[]{:S(2)}, u32[]{:S(2)}) collective-permute-start(bf16[64,1536]{1,0:T(8,128)(2,1)} %bitcast.12), channel_id=1, source_target_pairs={{0,4},{4,0},{8,12},{12,8},{1,5},{5,1},{9,13},{13,9},{2,6},{6,2},{1... | collective-permute-start | bytes 589832 | tf_op jit(solution)/shard_map/ppermute | solution.py:84
  5.6 7.9 %collective-permute-done.two_ref = bf16[64,1536]{1,0:T(8,128)(2,1)S(1)} collective-permute-done((bf16[64,1536]{1,0:T(8,128)(2,1)}, bf16[64,1536]{1,0:T(8,128)(2,1)S(1)}, u32[]{:S(2)}, u32[]{:S(2)}) %collective-permute-start) | collective-permute-done | bytes 196640 | tf_op jit(solution)/shard_map/ppermute | solution.py:84
  13.5 0.7 %collective-permute-start.1 = (bf16[64,1536]{1,0:T(8,128)(2,1)S(1)}, bf16[64,1536]{1,0:T(8,128)(2,1)S(1)}, u32[]{:S(2)}, u32[]{:S(2)}) collective-permute-start(bf16[64,1536]{1,0:T(8,128)(2,1)S(1)} %collective-permute-done.two_ref), channel_id=1, source_target_pairs={{0,4},{4,0},{8,12},{12,8},{1,5},{5,1},{9,13},{13,9},{2,6},{6,2},{1... | collective-permute-start | bytes 589832 | tf_op jit(solution)/shard_map/ppermute | solution.py:84
  14.2 0.0 copy-start
  14.2 1.9 %copy-done = bf16[12,8,128,128]{3,2,1,0:T(8,128)(2,1)S(1)} copy-done((bf16[12,8,128,128]{3,2,1,0:T(8,128)(2,1)S(1)}, bf16[12,8,128,128]{3,2,1,0:T(8,128)(2,1)}, u32[]{:S(2)}) %copy-start) | copy-done | bytes 3145752
  16.1 0.0 copy-start.2
  16.1 0.9 %copy-done.2 = bf16[1536,64]{0,1:T(8,128)(2,1)S(1)} copy-done((bf16[1536,64]{0,1:T(8,128)(2,1)S(1)}, bf16[1536,64]{0,1:T(8,128)(2,1)}, u32[]{:S(2)}) %copy-start.2) | copy-done | bytes 196632
  17.0 0.0 copy-start.4
  17.0 0.7 %copy-done.4 = s32[12,8]{0,1:T(8,128)S(1)} copy-done((s32[12,8]{0,1:T(8,128)S(1)}, s32[12,8]{0,1:T(8,128)}, u32[]{:S(2)}) %copy-start.4) | copy-done | bytes 408
  17.7 0.0 copy-start.1
  17.7 1.9 %own.1 = (f32[12,64,128]{2,1,0:T(8,128)S(1)}, s32[3,28]{1,0:T(4,128)S(1)}) custom-call(s32[1]{0:T(128)} %bitcast.3.me_ref, s32[8,12]{1,0:T(8,128)S(1)} %bitcast.15, bf16[64,1536]{1,0:T(8,128)(2,1)S(1)} %bitcast.13, bf16[96,128,128]{2,1,0:T(8,128)(2,1)S(1)} %bitcast.8), custom_call_target="tpu_custom_call" | custom-call | flops 25165824 | bytes 6291456 | tf_op jit(solution)/shard_map/own/pallas_call | solution.py:102
  19.6 0.0 collective-permute-done.2.one_ref
  19.6 0.0 copy-done.1
  19.6 0.0 copy-start.5
  19.6 0.0 copy-start.3
  19.7 1.9 %middle.1.acc_in = f32[12,64,128]{2,1,0:T(8,128)S(1)} custom-call(s32[3,28]{1,0:T(4,128)S(1)} %get-tuple-element.11.list_ref, bf16[64,1536]{1,0:T(8,128)(2,1)S(1)} %collective-permute-done.2.one_ref, bf16[64,1536]{1,0:T(8,128)(2,1)S(1)} %collective-permute-done.two_ref, bf16[96,128,128]{2,1,0:T(8,128)(2,1)S(1)} %bitcast.9, ...), custom_call_target="tpu_custom_call", output_to_operand_aliasing={{}: (4, {})} | custom-call | flops 117440512 | bytes 6291456 | tf_op jit(solution)/shard_map/middle/pallas_call | solution.py:117
  21.6 0.0 collective-permute-done.1.three_ref
  21.6 1.3 %last.1 = (f32[12,64,128]{2,1,0:T(8,128)S(1)}, bf16[64,384]{1,0:T(8,128)(2,1)S(1)}, bf16[64,384]{1,0:T(8,128)(2,1)S(1)}, bf16[64,384]{1,0:T(8,128)(2,1)S(1)}, bf16[64,384]{1,0:T(8,128)(2,1)S(1)}) custom-call(s32[1]{0:T(128)} %bitcast.feat_ref, s32[3,28]{1,0:T(4,128)S(1)} %get-tuple-element.11.list_ref, ...), custom_call_target="tpu_custom_call", output_to_operand_aliasing={{0}: (4, {})} | custom-call | flops 58720256 | bytes 1572864 | tf_op jit(solution)/shard_map/last/pallas_call | solution.py:130
  23.0 0.1 collective-permute-start.3
  23.0 1.6 %collective-permute-start.4 = (bf16[64,384]{1,0:T(8,128)(2,1)S(1)}, bf16[64,384]{1,0:T(8,128)(2,1)S(1)}, u32[]{:S(2)}, u32[]{:S(2)}) collective-permute-start(bf16[64,384]{1,0:T(8,128)(2,1)S(1)} %get-tuple-element.15), channel_id=1, source_target_pairs={{0,2},{1,3},{2,0},{3,1},{4,6},{5,7},{6,4},{7,5},{8,10},{9,11},{10,... | collective-permute-start | bytes 147464 | tf_op jit(solution)/shard_map/ppermute | solution.py:84
  24.6 0.3 %collective-permute-start.5 = (bf16[64,384]{1,0:T(8,128)(2,1)S(1)}, bf16[64,384]{1,0:T(8,128)(2,1)S(1)}, u32[]{:S(2)}, u32[]{:S(2)}) collective-permute-start(bf16[64,384]{1,0:T(8,128)(2,1)S(1)} %get-tuple-element.16), channel_id=1, source_target_pairs={{0,3},{1,2},{2,1},{3,0},{4,7},{5,6},{6,5},{7,4},{8,11},{9,10},{10,... | collective-permute-start | bytes 147464 | tf_op jit(solution)/shard_map/ppermute | solution.py:84
  24.9 0.0 copy-done.5
  24.9 0.1 copy.8.bias_ref
  25.0 0.0 collective-permute-done.3.refs_1_
  25.0 2.2 %collective-permute-done.4.refs_2_ = bf16[64,384]{1,0:T(8,128)(2,1)S(1)} collective-permute-done((bf16[64,384]{1,0:T(8,128)(2,1)S(1)}, bf16[64,384]{1,0:T(8,128)(2,1)S(1)}, u32[]{:S(2)}, u32[]{:S(2)}) %collective-permute-start.4) | collective-permute-done | bytes 49184 | tf_op jit(solution)/shard_map/ppermute | solution.py:84
  27.2 1.1 %collective-permute-done.5.refs_3_ = bf16[64,384]{1,0:T(8,128)(2,1)S(1)} collective-permute-done((bf16[64,384]{1,0:T(8,128)(2,1)S(1)}, bf16[64,384]{1,0:T(8,128)(2,1)S(1)}, u32[]{:S(2)}, u32[]{:S(2)}) %collective-permute-start.5) | collective-permute-done | bytes 49184 | tf_op jit(solution)/shard_map/ppermute | solution.py:84
  28.3 0.0 copy-done.3
  28.3 0.9 %project.1 = bf16[172,384]{1,0:T(8,128)(2,1)} custom-call(s32[1]{0:T(128)} %bitcast.feat_ref, bf16[172,256]{1,0:T(8,128)(2,1)S(1)} %bitcast.14, f32[172,1]{1,0:T(8,128)S(1)} %copy.8.bias_ref, bf16[64,384]{1,0:T(8,128)(2,1)S(1)} %get-tuple-element.13.refs_0_, bf16[64,384]{1,0:T(8,128)(2,1)S(1)} %collective-permute-done.3.refs_1_, ...), custom_call_target="tpu_custom_call" | custom-call | tf_op jit(solution)/shard_map/project/pallas_call | solution.py:145
Async XLA Ops:
  0.0 13.5 %collective-permute-start = (bf16[64,1536]{1,0:T(8,128)(2,1)}, bf16[64,1536]{1,0:T(8,128)(2,1)S(1)}, u32[]{:S(2)}, u32[]{:S(2)}) collective-permute-start(bf16[64,1536]{1,0:T(8,128)(2,1)} %bitcast.11), channel_id=1, source_target_pairs={{0,8},{4,12},{8,0},{12,4},{1,9},{5,13},{9,1},{13,5},{2,10},{6,14},... | collective-permute-start | bytes 589832 | tf_op jit(solution)/shard_map/ppermute | solution.py:84
  4.0 15.6 %collective-permute-start.2 = (bf16[64,1536]{1,0:T(8,128)(2,1)}, bf16[64,1536]{1,0:T(8,128)(2,1)S(1)}, u32[]{:S(2)}, u32[]{:S(2)}) collective-permute-start(bf16[64,1536]{1,0:T(8,128)(2,1)} %bitcast.12), channel_id=1, source_target_pairs={{0,4},{4,0},{8,12},{12,8},{1,5},{5,1},{9,13},{13,9},{2,6},{6,2},{1... | collective-permute-start | bytes 589832 | tf_op jit(solution)/shard_map/ppermute | solution.py:84
  13.5 8.1 %collective-permute-start.1 = (bf16[64,1536]{1,0:T(8,128)(2,1)S(1)}, bf16[64,1536]{1,0:T(8,128)(2,1)S(1)}, u32[]{:S(2)}, u32[]{:S(2)}) collective-permute-start(bf16[64,1536]{1,0:T(8,128)(2,1)S(1)} %collective-permute-done.two_ref), channel_id=1, source_target_pairs={{0,4},{4,0},{8,12},{12,8},{1,5},{5,1},{9,13},{13,9},{2,6},{6,2},{1... | collective-permute-start | bytes 589832 | tf_op jit(solution)/shard_map/ppermute | solution.py:84
  14.2 1.9 %copy-start = (bf16[12,8,128,128]{3,2,1,0:T(8,128)(2,1)S(1)}, bf16[12,8,128,128]{3,2,1,0:T(8,128)(2,1)}, u32[]{:S(2)}) copy-start(bf16[12,8,128,128]{3,2,1,0:T(8,128)(2,1)} %param.6) | copy-start | bytes 9437188
  16.1 0.9 %copy-start.2 = (bf16[1536,64]{0,1:T(8,128)(2,1)S(1)}, bf16[1536,64]{0,1:T(8,128)(2,1)}, u32[]{:S(2)}) copy-start(bf16[1536,64]{0,1:T(8,128)(2,1)} %param.5) | copy-start | bytes 589828
  17.0 0.7 %copy-start.4 = (s32[12,8]{0,1:T(8,128)S(1)}, s32[12,8]{0,1:T(8,128)}, u32[]{:S(2)}) copy-start(s32[12,8]{0,1:T(8,128)} %param.7) | copy-start | bytes 1156
  17.7 1.9 %copy-start.1 = (bf16[12,8,128,128]{3,2,1,0:T(8,128)(2,1)S(1)}, bf16[12,8,128,128]{3,2,1,0:T(8,128)(2,1)}, u32[]{:S(2)}) copy-start(bf16[12,8,128,128]{3,2,1,0:T(8,128)(2,1)} %param.6) | copy-start | bytes 9437188
  19.6 5.3 %copy-start.5 = (f32[172]{0:T(256)S(1)}, f32[172]{0:T(256)}, u32[]{:S(2)}) copy-start(f32[172]{0:T(256)} %param.9) | copy-start | bytes 2068
  19.6 8.6 %copy-start.3 = (bf16[256,172]{0,1:T(8,128)(2,1)S(1)}, bf16[256,172]{0,1:T(8,128)(2,1)}, u32[]{:S(2)}) copy-start(bf16[256,172]{0,1:T(8,128)(2,1)} %param.8) | copy-start | bytes 264196
  23.0 2.1 %collective-permute-start.3 = (bf16[64,384]{1,0:T(8,128)(2,1)S(1)}, bf16[64,384]{1,0:T(8,128)(2,1)S(1)}, u32[]{:S(2)}, u32[]{:S(2)}) collective-permute-start(bf16[64,384]{1,0:T(8,128)(2,1)S(1)} %get-tuple-element.14), channel_id=1, source_target_pairs={{0,1},{1,0},{2,3},{3,2},{4,5},{5,4},{6,7},{7,6},{8,9},{9,8},{10,11... | collective-permute-start | bytes 147464 | tf_op jit(solution)/shard_map/ppermute | solution.py:84
  23.0 4.2 %collective-permute-start.4 = (bf16[64,384]{1,0:T(8,128)(2,1)S(1)}, bf16[64,384]{1,0:T(8,128)(2,1)S(1)}, u32[]{:S(2)}, u32[]{:S(2)}) collective-permute-start(bf16[64,384]{1,0:T(8,128)(2,1)S(1)} %get-tuple-element.15), channel_id=1, source_target_pairs={{0,2},{1,3},{2,0},{3,1},{4,6},{5,7},{6,4},{7,5},{8,10},{9,11},{10,... | collective-permute-start | bytes 147464 | tf_op jit(solution)/shard_map/ppermute | solution.py:84
  24.6 3.7 %collective-permute-start.5 = (bf16[64,384]{1,0:T(8,128)(2,1)S(1)}, bf16[64,384]{1,0:T(8,128)(2,1)S(1)}, u32[]{:S(2)}, u32[]{:S(2)}) collective-permute-start(bf16[64,384]{1,0:T(8,128)(2,1)S(1)} %get-tuple-element.16), channel_id=1, source_target_pairs={{0,3},{1,2},{2,1},{3,0},{4,7},{5,6},{6,5},{7,4},{8,11},{9,10},{10,... | collective-permute-start | bytes 147464 | tf_op jit(solution)/shard_map/ppermute | solution.py:84

commit v2 on v1

--- a/solution.py
+++ b/solution.py
@@ -8,6 +8,7 @@
 from jax.sharding import PartitionSpec as P
 
 VMEM = pl.BlockSpec(memory_space=pltpu.VMEM)
+HBM = pl.BlockSpec(memory_space=pltpu.HBM)
 SMEM = pl.BlockSpec(memory_space=pltpu.SMEM)
 
 
@@ -17,11 +18,18 @@
     )
 
 
-def own_kernel(me_ref, col_ref, x_ref, tiles_ref, acc_ref, list_ref, count):
+def own_kernel(
+    me_ref, col_ref, x_hbm, tiles_hbm, acc_ref, list_ref, x_ref, tiles_ref, count, sems
+):
     slot_count, stripe_blocks = col_ref.shape
     size = tiles_ref.shape[-1]
-    sources, _ = list_ref.shape
-    for source in range(sources):
+    copies = [
+        pltpu.make_async_copy(x_hbm, x_ref, sems.at[0]),
+        pltpu.make_async_copy(tiles_hbm.at[:, 0], tiles_ref, sems.at[1]),
+    ]
+    for copy in copies:
+        copy.start()
+    for source in range(list_ref.shape[0]):
         count[source] = 0
     for row in range(stripe_blocks):
         for slot in range(1, slot_count):
@@ -33,33 +41,47 @@
                 column - stripe * stripe_blocks
             )
             count[which] = at + 1
+    for copy in copies:
+        copy.wait()
     for row in range(stripe_blocks):
-        acc_ref[row] = times_tile(
-            x_ref[:, row * size : (row + 1) * size], tiles_ref[row * slot_count]
-        )
-
-
-def add_slots(which, list_ref, x_ref, tiles_ref, acc_ref):
+        acc_ref[row] = times_tile(x_ref[:, row * size : (row + 1) * size], tiles_ref[row])
+
+
+def add_slots(which, list_ref, x_ref, tiles, acc_ref, slot_count):
     stripe_blocks = acc_ref.shape[0]
-    slot_count = tiles_ref.shape[0] // stripe_blocks
-    size = tiles_ref.shape[-1]
+    size = tiles.shape[-1]
     for entry in range(list_ref.shape[1]):
         code = list_ref[which, entry]
         slot = lax.div(code, stripe_blocks)
         column = code - slot * stripe_blocks
         block = x_ref[:, pl.ds(pl.multiple_of(column * size, size), size)]
-        acc_ref[lax.div(slot, slot_count)] += times_tile(block, tiles_ref[slot])
-
-
-def middle_kernel(list_ref, one_ref, two_ref, tiles_ref, acc_in, acc_ref):
+        acc_ref[lax.div(slot, slot_count)] += times_tile(block, tiles[entry])
+
+
+def middle_kernel(
+    list_ref, one_ref, two_ref, tiles_hbm, acc_in, acc_ref, three_tiles, tiles_ref, sems
+):
     del acc_in
-    add_slots(0, list_ref, one_ref, tiles_ref, acc_ref)
-    add_slots(1, list_ref, two_ref, tiles_ref, acc_ref)
-
-
-def last_kernel(feat_ref, list_ref, three_ref, tiles_ref, acc_in, acc_ref, *part_refs):
+    stripe_blocks, slot_count = tiles_hbm.shape[:2]
+    slots = list_ref.shape[1]
+    places = [tiles_ref.at[0], tiles_ref.at[1], three_tiles]
+    for which, place in enumerate(places):
+        for entry in range(slots):
+            slot = lax.div(list_ref[which, entry], stripe_blocks)
+            row = lax.div(slot, slot_count)
+            pltpu.make_async_copy(
+                tiles_hbm.at[row, slot - row * slot_count], place.at[entry], sems.at[which]
+            ).start()
+    for which, x_ref in enumerate([one_ref, two_ref]):
+        place = places[which]
+        pltpu.make_async_copy(place, place, sems.at[which]).wait()
+        add_slots(which, list_ref, x_ref, place, acc_ref, slot_count)
+    pltpu.make_async_copy(three_tiles, three_tiles, sems.at[2]).wait()
+
+
+def last_kernel(slot_count, feat_ref, list_ref, three_ref, tiles_ref, acc_in, acc_ref, *part_refs):
     del acc_in
-    add_slots(2, list_ref, three_ref, tiles_ref, acc_ref)
+    add_slots(2, list_ref, three_ref, tiles_ref, acc_ref, slot_count)
     size = tiles_ref.shape[-1]
     share = acc_ref.shape[0] // len(part_refs)
     for k, part_ref in enumerate(part_refs):
@@ -78,6 +100,14 @@
         rows[pl.ds(pl.multiple_of(owner * width, width), width), :] = part_ref[...]
     total = jnp.dot(weight_ref[...], rows[...], preferred_element_type=jnp.float32)
     out_ref[...] = (total + bias_ref[...]).astype(out_ref.dtype)
+
+
+def in_hbm(x):
+    return pltpu.with_memory_space_constraint(x, pltpu.HBM)
+
+
+def in_vmem(*arrays):
+    return [pltpu.with_memory_space_constraint(x, pltpu.VMEM) for x in arrays]
 
 
 def exchange(x, axis, size, bit):
@@ -93,53 +123,62 @@
     x = features.T
     two = exchange(x, "node", stripes, 2)
     one = exchange(x, "node", stripes, 1)
-    three = exchange(two, "node", stripes, 1)
-
-    params = pltpu.CompilerParams(vmem_limit_bytes=32 << 20)
-    acc_shape = jax.ShapeDtypeStruct((stripe_blocks, width, size), jnp.float32)
-    flat = tiles.reshape(-1, size, size)
+
+    params = pltpu.CompilerParams(vmem_limit_bytes=12 << 20)
+    acc_shape = pltpu.VMEM((stripe_blocks, width, size), jnp.float32)
     tile_flops = 2 * size * size * width
+    held = pltpu.VMEM((remote, size, size), tiles.dtype)
     acc, lists = pl.pallas_call(
         own_kernel,
-        out_shape=(
-            acc_shape,
-            jax.ShapeDtypeStruct((stripes - 1, remote), jnp.int32),
-        ),
-        in_specs=[SMEM, SMEM, VMEM, VMEM],
+        out_shape=(acc_shape, jax.ShapeDtypeStruct((stripes - 1, remote), jnp.int32)),
+        in_specs=[SMEM, SMEM, HBM, HBM],
         out_specs=(VMEM, SMEM),
-        scratch_shapes=[pltpu.SMEM((stripes - 1,), jnp.int32)],
+        scratch_shapes=[
+            pltpu.VMEM(x.shape, x.dtype),
+            pltpu.VMEM((stripe_blocks, size, size), tiles.dtype),
+            pltpu.SMEM((stripes - 1,), jnp.int32),
+            pltpu.SemaphoreType.DMA((2,)),
+        ],
         compiler_params=params,
         cost_estimate=pl.CostEstimate(
-            flops=stripe_blocks * tile_flops, bytes_accessed=flat.size * 4, transcendentals=0
+            flops=stripe_blocks * tile_flops, bytes_accessed=tiles.size, transcendentals=0
         ),
         name="own",
-    )(me, col_block.T, x, flat)
-    acc = pl.pallas_call(
+    )(me, col_block.T, in_hbm(x), in_hbm(tiles))
+    ready, acc = lax.optimization_barrier((two, acc))
+    three = exchange(ready, "node", stripes, 1)
+    acc, three_tiles = pl.pallas_call(
         middle_kernel,
-        out_shape=acc_shape,
-        in_specs=[SMEM, VMEM, VMEM, VMEM, VMEM],
-        out_specs=VMEM,
+        out_shape=(acc_shape, held),
+        in_specs=[SMEM, VMEM, VMEM, HBM, VMEM],
+        out_specs=(VMEM, VMEM),
         input_output_aliases={4: 0},
+        scratch_shapes=[
+            pltpu.VMEM((2,) + held.shape, held.dtype),
+            pltpu.SemaphoreType.DMA((3,)),
+        ],
         compiler_params=params,
         cost_estimate=pl.CostEstimate(
-            flops=2 * remote * tile_flops, bytes_accessed=flat.size * 4, transcendentals=0
+            flops=2 * remote * tile_flops, bytes_accessed=tiles.size * 4, transcendentals=0
         ),
         name="middle",
-    )(lists, one, two, flat, acc)
-    part_shape = jax.ShapeDtypeStruct((width, stripe_blocks // slices * size), jnp.bfloat16)
+    )(lists, *in_vmem(one, ready), in_hbm(tiles), *in_vmem(acc))
+    part_shape = pltpu.VMEM((width, stripe_blocks // slices * size), jnp.bfloat16)
     _, *parts = pl.pallas_call(
-        last_kernel,
+        functools.partial(last_kernel, slot_count),
         out_shape=(acc_shape,) + (part_shape,) * slices,
         in_specs=[SMEM, SMEM, VMEM, VMEM, VMEM],
         out_specs=(VMEM,) * (1 + slices),
         input_output_aliases={4: 0},
         compiler_params=params,
         cost_estimate=pl.CostEstimate(
-            flops=remote * tile_flops, bytes_accessed=flat.size, transcendentals=0
+            flops=remote * tile_flops, bytes_accessed=tiles.size, transcendentals=0
         ),
         name="last",
-    )(feat, lists, three, flat, acc)
-    parts = parts[:1] + [exchange(parts[k], "feat", slices, k) for k in range(1, slices)]
+    )(feat, lists, *in_vmem(three, three_tiles, acc))
+    parts = parts[:1] + [
+        exchange(parts[k], "feat", slices, k) for k in range(1, slices)
+    ]
     rows = part_shape.shape[1]
     classes = weight.shape[1]
     logits = pl.pallas_call(
@@ -150,7 +189,7 @@
         scratch_shapes=[pltpu.VMEM((slices * width, rows), jnp.bfloat16)],
         compiler_params=params,
         name="project",
-    )(feat, weight.T, bias[:, None], *parts)
+    )(feat, *in_vmem(weight.T, bias[:, None], *parts))
     return logits.T
 
 
@@ -169,7 +208,7 @@
 
 def solution(mesh):
     stripes, slices = mesh.shape["node"], mesh.shape["feat"]
-    line = stripes == 4 and slices & (slices - 1) == 0
+    line = stripes == 4 and slices > 1 and slices & (slices - 1) == 0
     body = functools.partial(on_line, stripes, slices) if line else on_device
     in_specs = (
         P(("groups", "node"), "feat"),

time: 29.4 us -> 27.1 us (0.922)
  local copies, waits for them, and re-layouts: 3.63 us -> 0.81 us
  Pallas kernels: 6.07 us -> 7.76 us
  waiting for transfers between devices: 11.1 us -> 9.91 us
    unnamed x12 -> x6, local copies, waits for them, and re-layouts: 3.52 us -> 0.7 us
    pallas_call x2, Pallas kernels: 3.27 us -> 4.55 us  [the longest x1 3.22 us: on_line(): pl.pallas_call(middle_kernel, out_shape=(acc_shape, held), in_specs=[SMEM...]
    ppermute x6, waiting for transfers between devices: 11.1 us -> 9.91 us  [exchange(): return lax.ppermute(x, axis, [(i, i ^ bit) for i in range(size)])]
    pallas_call x1, Pallas kernels: 1.91 us -> 2.34 us  [on_line(): pl.pallas_call(own_kernel, out_shape=(acc_shape, jax.ShapeDtypeStruct((st...]
  transfers between devices with their start and end apart: 6 -> 6, of which waited for: 3 -> 4; matrix products, arithmetic and copies ran while one was open for 0% -> 0% of each run, Pallas kernels for 13% -> 21%
where the time goes in v2:
time: 27.1 us; the launch traced here: 26.8 us
  waiting for transfers between devices  9.91 us (37%)
  starting transfers between devices  8.27 us (31%)
  Pallas kernels  7.76 us (29%)
  local copies, waits for them, and re-layouts  0.81 us (3%)
    ppermute x6, waiting for transfers between devices, exchange(): return lax.ppermute(x, axis, [(i, i ^ bit) for i in range(size)])  9.91 us
    ppermute x6, starting transfers between devices, exchange(): return lax.ppermute(x, axis, [(i, i ^ bit) for i in range(size)])  8.27 us
    pallas_call x1, Pallas kernels, on_line(): pl.pallas_call(middle_kernel, out_shape=(acc_shape, held), in_specs=[SMEM...  3.22 us
    pallas_call x1, Pallas kernels, on_line(): pl.pallas_call(own_kernel, out_shape=(acc_shape, jax.ShapeDtypeStruct((st...  2.34 us
    pallas_call x1, Pallas kernels, on_line(): pl.pallas_call(functools.partial(last_kernel, slot_count), out_shape=(acc...  1.32 us
    pallas_call x1, Pallas kernels, on_line(): pl.pallas_call(project_kernel, out_shape=jax.ShapeDtypeStruct((classes, r...  0.88 us
    unnamed x6, local copies, waits for them, and re-layouts  0.7 us
  transfers between devices with their start and end apart: 6, of which 4 were waited for; matrix products, arithmetic and copies ran while one was open for 0% of the time, Pallas kernels for 21%

profile of v2, /device:TPU:0, one launch (start us, length us, event | category | flops | bytes accessed | tf_op | source)
XLA Modules:
  0.0 26.8 jit_solution(13995302847516807834)
XLA Ops:
  0.0 4.0 %collective-permute-start = (bf16[64,1536]{1,0:T(8,128)(2,1)}, bf16[64,1536]{1,0:T(8,128)(2,1)S(1)}, u32[]{:S(2)}, u32[]{:S(2)}) collective-permute-start(bf16[64,1536]{1,0:T(8,128)(2,1)} %bitcast.9), channel_id=1, source_target_pairs={{0,8},{4,12},{8,0},{12,4},{1,9},{5,13},{9,1},{13,5},{2,10},{6,14},... | collective-permute-start | bytes 589832 | tf_op jit(solution)/shard_map/ppermute | solution.py:114
  4.0 1.6 %collective-permute-start.2 = (bf16[64,1536]{1,0:T(8,128)(2,1)}, bf16[64,1536]{1,0:T(8,128)(2,1)S(1)}, u32[]{:S(2)}, u32[]{:S(2)}) collective-permute-start(bf16[64,1536]{1,0:T(8,128)(2,1)} %bitcast.10), channel_id=1, source_target_pairs={{0,4},{4,0},{8,12},{12,8},{1,5},{5,1},{9,13},{13,9},{2,6},{6,2},{1... | collective-permute-start | bytes 589832 | tf_op jit(solution)/shard_map/ppermute | solution.py:114
  5.6 0.0 copy-start.1
  5.6 0.7 %copy-done.1 = s32[12,8]{0,1:T(8,128)S(1)} copy-done((s32[12,8]{0,1:T(8,128)S(1)}, s32[12,8]{0,1:T(8,128)}, u32[]{:S(2)}) %copy-start.1) | copy-done | bytes 408
  6.3 2.3 %own.1 = (f32[12,64,128]{2,1,0:T(8,128)S(1)}, s32[3,28]{1,0:T(4,128)S(1)}) custom-call(s32[1]{0:T(128)} %bitcast.3.me_ref, s32[8,12]{1,0:T(8,128)S(1)} %bitcast.8, bf16[64,1536]{1,0:T(8,128)(2,1)} %bitcast.11, bf16[12,8,128,128]{3,2,1,0:T(8,128)(2,1)} %tiles_hbm.3), custom_call_target="tpu_custom_call" | custom-call | flops 25165824 | bytes 1572864 | tf_op jit(solution)/shard_map/own/pallas_call | solution.py:131
  8.6 0.0 copy-start.2
  8.7 0.0 copy-start
  8.7 4.8 %collective-permute-done.two_ref = bf16[64,1536]{1,0:T(8,128)(2,1)S(1)} collective-permute-done((bf16[64,1536]{1,0:T(8,128)(2,1)}, bf16[64,1536]{1,0:T(8,128)(2,1)S(1)}, u32[]{:S(2)}, u32[]{:S(2)}) %collective-permute-start) | collective-permute-done | bytes 196640 | tf_op jit(solution)/shard_map/ppermute | solution.py:114
  13.5 0.7 %collective-permute-start.1 = (bf16[64,1536]{1,0:T(8,128)(2,1)S(1)}, bf16[64,1536]{1,0:T(8,128)(2,1)S(1)}, u32[]{:S(2)}, u32[]{:S(2)}) collective-permute-start(bf16[64,1536]{1,0:T(8,128)(2,1)S(1)} %collective-permute-done.two_ref), channel_id=1, source_target_pairs={{0,4},{4,0},{8,12},{12,8},{1,5},{5,1},{9,13},{13,9},{2,6},{6,2},{1... | collective-permute-start | bytes 589832 | tf_op jit(solution)/shard_map/ppermute | solution.py:114
  14.2 0.0 collective-permute-done.2.one_ref
  14.2 3.2 %middle.1 = (f32[12,64,128]{2,1,0:T(8,128)S(1)}, bf16[28,128,128]{2,1,0:T(8,128)(2,1)S(1)}) custom-call(s32[3,28]{1,0:T(4,128)S(1)} %get-tuple-element.15.list_ref, bf16[64,1536]{1,0:T(8,128)(2,1)S(1)} %collective-permute-done.2.one_ref, bf16[64,1536]{1,0:T(8,128)(2,1)S(1)} %collective-permute-done.two_ref, ...), custom_call_target="tpu_custom_call", output_to_operand_aliasing={{0}: (4, {})} | custom-call | flops 117440512 | bytes 6291456 | tf_op jit(solution)/shard_map/middle/pallas_call | solution.py:150
  17.4 2.1 %collective-permute-done.1.three_ref = bf16[64,1536]{1,0:T(8,128)(2,1)S(1)} collective-permute-done((bf16[64,1536]{1,0:T(8,128)(2,1)S(1)}, bf16[64,1536]{1,0:T(8,128)(2,1)S(1)}, u32[]{:S(2)}, u32[]{:S(2)}) %collective-permute-start.1) | collective-permute-done | bytes 196640 | tf_op jit(solution)/shard_map/ppermute | solution.py:114
  19.5 1.3 %last.1 = (f32[12,64,128]{2,1,0:T(8,128)S(1)}, bf16[64,384]{1,0:T(8,128)(2,1)S(1)}, bf16[64,384]{1,0:T(8,128)(2,1)S(1)}, bf16[64,384]{1,0:T(8,128)(2,1)S(1)}, bf16[64,384]{1,0:T(8,128)(2,1)S(1)}) custom-call(s32[1]{0:T(128)} %bitcast.feat_ref, s32[3,28]{1,0:T(4,128)S(1)} %get-tuple-element.15.list_ref, ...), custom_call_target="tpu_custom_call", output_to_operand_aliasing={{0}: (4, {})} | custom-call | flops 58720256 | bytes 1572864 | tf_op jit(solution)/shard_map/last/pallas_call | solution.py:167
  20.8 0.1 collective-permute-start.3
  20.9 1.3 %collective-permute-start.4 = (bf16[64,384]{1,0:T(8,128)(2,1)S(1)}, bf16[64,384]{1,0:T(8,128)(2,1)S(1)}, u32[]{:S(2)}, u32[]{:S(2)}) collective-permute-start(bf16[64,384]{1,0:T(8,128)(2,1)S(1)} %get-tuple-element.23), channel_id=1, source_target_pairs={{0,2},{1,3},{2,0},{3,1},{4,6},{5,7},{6,4},{7,5},{8,10},{9,11},{10,... | collective-permute-start | bytes 147464 | tf_op jit(solution)/shard_map/ppermute | solution.py:114
  22.2 0.5 %collective-permute-start.5 = (bf16[64,384]{1,0:T(8,128)(2,1)S(1)}, bf16[64,384]{1,0:T(8,128)(2,1)S(1)}, u32[]{:S(2)}, u32[]{:S(2)}) collective-permute-start(bf16[64,384]{1,0:T(8,128)(2,1)S(1)} %get-tuple-element.24), channel_id=1, source_target_pairs={{0,3},{1,2},{2,1},{3,0},{4,7},{5,6},{6,5},{7,4},{8,11},{9,10},{10,... | collective-permute-start | bytes 147464 | tf_op jit(solution)/shard_map/ppermute | solution.py:114
  22.8 0.0 copy-done.2
  22.8 0.1 copy.8.bias_ref
  22.9 0.0 collective-permute-done.3.refs_1_
  22.9 2.2 %collective-permute-done.4.refs_2_ = bf16[64,384]{1,0:T(8,128)(2,1)S(1)} collective-permute-done((bf16[64,384]{1,0:T(8,128)(2,1)S(1)}, bf16[64,384]{1,0:T(8,128)(2,1)S(1)}, u32[]{:S(2)}, u32[]{:S(2)}) %collective-permute-start.4) | collective-permute-done | bytes 49184 | tf_op jit(solution)/shard_map/ppermute | solution.py:114
  25.1 0.9 %collective-permute-done.5.refs_3_ = bf16[64,384]{1,0:T(8,128)(2,1)S(1)} collective-permute-done((bf16[64,384]{1,0:T(8,128)(2,1)S(1)}, bf16[64,384]{1,0:T(8,128)(2,1)S(1)}, u32[]{:S(2)}, u32[]{:S(2)}) %collective-permute-start.5) | collective-permute-done | bytes 49184 | tf_op jit(solution)/shard_map/ppermute | solution.py:114
  25.9 0.0 copy-done
  25.9 0.9 %project.1 = bf16[172,384]{1,0:T(8,128)(2,1)} custom-call(s32[1]{0:T(128)} %bitcast.feat_ref, bf16[172,256]{1,0:T(8,128)(2,1)S(1)} %bitcast.7, f32[172,1]{1,0:T(8,128)S(1)} %copy.8.bias_ref, bf16[64,384]{1,0:T(8,128)(2,1)S(1)} %get-tuple-element.21.refs_0_, bf16[64,384]{1,0:T(8,128)(2,1)S(1)} %collective-permute-done.3.refs_1_, ...), custom_call_target="tpu_custom_call" | custom-call | tf_op jit(solution)/shard_map/project/pallas_call | solution.py:184
Async XLA Ops:
  0.0 13.5 %collective-permute-start = (bf16[64,1536]{1,0:T(8,128)(2,1)}, bf16[64,1536]{1,0:T(8,128)(2,1)S(1)}, u32[]{:S(2)}, u32[]{:S(2)}) collective-permute-start(bf16[64,1536]{1,0:T(8,128)(2,1)} %bitcast.9), channel_id=1, source_target_pairs={{0,8},{4,12},{8,0},{12,4},{1,9},{5,13},{9,1},{13,5},{2,10},{6,14},... | collective-permute-start | bytes 589832 | tf_op jit(solution)/shard_map/ppermute | solution.py:114
  4.0 10.2 %collective-permute-start.2 = (bf16[64,1536]{1,0:T(8,128)(2,1)}, bf16[64,1536]{1,0:T(8,128)(2,1)S(1)}, u32[]{:S(2)}, u32[]{:S(2)}) collective-permute-start(bf16[64,1536]{1,0:T(8,128)(2,1)} %bitcast.10), channel_id=1, source_target_pairs={{0,4},{4,0},{8,12},{12,8},{1,5},{5,1},{9,13},{13,9},{2,6},{6,2},{1... | collective-permute-start | bytes 589832 | tf_op jit(solution)/shard_map/ppermute | solution.py:114
  5.6 0.7 %copy-start.1 = (s32[12,8]{0,1:T(8,128)S(1)}, s32[12,8]{0,1:T(8,128)}, u32[]{:S(2)}) copy-start(s32[12,8]{0,1:T(8,128)} %param.7) | copy-start | bytes 1156
  8.6 14.1 %copy-start.2 = (f32[172]{0:T(256)S(1)}, f32[172]{0:T(256)}, u32[]{:S(2)}) copy-start(f32[172]{0:T(256)} %param.9) | copy-start | bytes 2068
  8.7 17.3 %copy-start = (bf16[256,172]{0,1:T(8,128)(2,1)S(1)}, bf16[256,172]{0,1:T(8,128)(2,1)}, u32[]{:S(2)}) copy-start(bf16[256,172]{0,1:T(8,128)(2,1)} %param.8) | copy-start | bytes 264196
  13.5 6.0 %collective-permute-start.1 = (bf16[64,1536]{1,0:T(8,128)(2,1)S(1)}, bf16[64,1536]{1,0:T(8,128)(2,1)S(1)}, u32[]{:S(2)}, u32[]{:S(2)}) collective-permute-start(bf16[64,1536]{1,0:T(8,128)(2,1)S(1)} %collective-permute-done.two_ref), channel_id=1, source_target_pairs={{0,4},{4,0},{8,12},{12,8},{1,5},{5,1},{9,13},{13,9},{2,6},{6,2},{1... | collective-permute-start | bytes 589832 | tf_op jit(solution)/shard_map/ppermute | solution.py:114
  20.8 2.1 %collective-permute-start.3 = (bf16[64,384]{1,0:T(8,128)(2,1)S(1)}, bf16[64,384]{1,0:T(8,128)(2,1)S(1)}, u32[]{:S(2)}, u32[]{:S(2)}) collective-permute-start(bf16[64,384]{1,0:T(8,128)(2,1)S(1)} %get-tuple-element.22), channel_id=1, source_target_pairs={{0,1},{1,0},{2,3},{3,2},{4,5},{5,4},{6,7},{7,6},{8,9},{9,8},{10,11... | collective-permute-start | bytes 147464 | tf_op jit(solution)/shard_map/ppermute | solution.py:114
  20.9 4.2 %collective-permute-start.4 = (bf16[64,384]{1,0:T(8,128)(2,1)S(1)}, bf16[64,384]{1,0:T(8,128)(2,1)S(1)}, u32[]{:S(2)}, u32[]{:S(2)}) collective-permute-start(bf16[64,384]{1,0:T(8,128)(2,1)S(1)} %get-tuple-element.23), channel_id=1, source_target_pairs={{0,2},{1,3},{2,0},{3,1},{4,6},{5,7},{6,4},{7,5},{8,10},{9,11},{10,... | collective-permute-start | bytes 147464 | tf_op jit(solution)/shard_map/ppermute | solution.py:114
  22.2 3.7 %collective-permute-start.5 = (bf16[64,384]{1,0:T(8,128)(2,1)S(1)}, bf16[64,384]{1,0:T(8,128)(2,1)S(1)}, u32[]{:S(2)}, u32[]{:S(2)}) collective-permute-start(bf16[64,384]{1,0:T(8,128)(2,1)S(1)} %get-tuple-element.24), channel_id=1, source_target_pairs={{0,3},{1,2},{2,1},{3,0},{4,7},{5,6},{6,5},{7,4},{8,11},{9,10},{10,... | collective-permute-start | bytes 147464 | tf_op jit(solution)/shard_map/ppermute | solution.py:114

commit v3 on v2

--- a/solution.py
+++ b/solution.py
@@ -47,7 +47,11 @@
         acc_ref[row] = times_tile(x_ref[:, row * size : (row + 1) * size], tiles_ref[row])
 
 
-def add_slots(which, list_ref, x_ref, tiles, acc_ref, slot_count):
+def times_turned(block_t, tile_t):
+    return jnp.dot(block_t, tile_t, preferred_element_type=jnp.float32)
+
+
+def add_slots(which, list_ref, x_ref, tiles, acc_ref, slot_count, times):
     stripe_blocks = acc_ref.shape[0]
     size = tiles.shape[-1]
     for entry in range(list_ref.shape[1]):
@@ -55,7 +59,7 @@
         slot = lax.div(code, stripe_blocks)
         column = code - slot * stripe_blocks
         block = x_ref[:, pl.ds(pl.multiple_of(column * size, size), size)]
-        acc_ref[lax.div(slot, slot_count)] += times_tile(block, tiles[entry])
+        acc_ref[lax.div(slot, slot_count)] += times(block, tiles[entry])
 
 
 def middle_kernel(
@@ -64,7 +68,7 @@
     del acc_in
     stripe_blocks, slot_count = tiles_hbm.shape[:2]
     slots = list_ref.shape[1]
-    places = [tiles_ref.at[0], tiles_ref.at[1], three_tiles]
+    places = [tiles_ref.at[0], tiles_ref.at[1], tiles_ref.at[2]]
     for which, place in enumerate(places):
         for entry in range(slots):
             slot = lax.div(list_ref[which, entry], stripe_blocks)
@@ -75,13 +79,15 @@
     for which, x_ref in enumerate([one_ref, two_ref]):
         place = places[which]
         pltpu.make_async_copy(place, place, sems.at[which]).wait()
-        add_slots(which, list_ref, x_ref, place, acc_ref, slot_count)
-    pltpu.make_async_copy(three_tiles, three_tiles, sems.at[2]).wait()
+        add_slots(which, list_ref, x_ref, place, acc_ref, slot_count, times_tile)
+    pltpu.make_async_copy(places[2], places[2], sems.at[2]).wait()
+    for entry in range(slots):
+        three_tiles[entry] = places[2][entry].T
 
 
 def last_kernel(slot_count, feat_ref, list_ref, three_ref, tiles_ref, acc_in, acc_ref, *part_refs):
     del acc_in
-    add_slots(2, list_ref, three_ref, tiles_ref, acc_ref, slot_count)
+    add_slots(2, list_ref, three_ref, tiles_ref, acc_ref, slot_count, times_turned)
     size = tiles_ref.shape[-1]
     share = acc_ref.shape[0] // len(part_refs)
     for k, part_ref in enumerate(part_refs):
@@ -154,7 +160,7 @@
         out_specs=(VMEM, VMEM),
         input_output_aliases={4: 0},
         scratch_shapes=[
-            pltpu.VMEM((2,) + held.shape, held.dtype),
+            pltpu.VMEM((3,) + held.shape, held.dtype),
             pltpu.SemaphoreType.DMA((3,)),
         ],
         compiler_params=params,

time: 27.1 us -> 26.7 us (0.985)
  waiting for transfers between devices: 9.91 us -> 9.62 us
    pallas_call x1, Pallas kernels: 1.32 us -> 0.98 us  [on_line(): pl.pallas_call(functools.partial(last_kernel, slot_count), out_shape=(acc...]
    ppermute x6, waiting for transfers between devices: 9.91 us -> 9.62 us  [exchange(): return lax.ppermute(x, axis, [(i, i ^ bit) for i in range(size)])]
    pallas_call x1, Pallas kernels: 3.22 us -> 3.51 us  [on_line(): pl.pallas_call(middle_kernel, out_shape=(acc_shape, held), in_specs=[SMEM...]
  transfers between devices with their start and end apart: 6 -> 6, of which waited for: 4 -> 4; matrix products, arithmetic and copies ran while one was open for 0% -> 0% of each run, Pallas kernels for 21% -> 22%
where the time goes in v3:
time: 26.7 us; the launch traced here: 26.5 us
  waiting for transfers between devices  9.62 us (36%)
  starting transfers between devices  8.27 us (31%)
  Pallas kernels  7.71 us (29%)
  local copies, waits for them, and re-layouts  0.81 us (3%)
    ppermute x6, waiting for transfers between devices, exchange(): return lax.ppermute(x, axis, [(i, i ^ bit) for i in range(size)])  9.62 us
    ppermute x6, starting transfers between devices, exchange(): return lax.ppermute(x, axis, [(i, i ^ bit) for i in range(size)])  8.27 us
    pallas_call x1, Pallas kernels, on_line(): pl.pallas_call(middle_kernel, out_shape=(acc_shape, held), in_specs=[SMEM...  3.51 us
    pallas_call x1, Pallas kernels, on_line(): pl.pallas_call(own_kernel, out_shape=(acc_shape, jax.ShapeDtypeStruct((st...  2.34 us
    pallas_call x1, Pallas kernels, on_line(): pl.pallas_call(functools.partial(last_kernel, slot_count), out_shape=(acc...  0.98 us
    pallas_call x1, Pallas kernels, on_line(): pl.pallas_call(project_kernel, out_shape=jax.ShapeDtypeStruct((classes, r...  0.88 us
    unnamed x6, local copies, waits for them, and re-layouts  0.7 us
  transfers between devices with their start and end apart: 6, of which 4 were waited for; matrix products, arithmetic and copies ran while one was open for 0% of the time, Pallas kernels for 22%

profile of v3, /device:TPU:0, one launch (start us, length us, event | category | flops | bytes accessed | tf_op | source)
XLA Modules:
  0.0 26.5 jit_solution(8486115068290633584)
XLA Ops:
  0.0 4.0 %collective-permute-start = (bf16[64,1536]{1,0:T(8,128)(2,1)}, bf16[64,1536]{1,0:T(8,128)(2,1)S(1)}, u32[]{:S(2)}, u32[]{:S(2)}) collective-permute-start(bf16[64,1536]{1,0:T(8,128)(2,1)} %bitcast.9), channel_id=1, source_target_pairs={{0,8},{4,12},{8,0},{12,4},{1,9},{5,13},{9,1},{13,5},{2,10},{6,14},... | collective-permute-start | bytes 589832 | tf_op jit(solution)/shard_map/ppermute | solution.py:120
  4.0 1.6 %collective-permute-start.2 = (bf16[64,1536]{1,0:T(8,128)(2,1)}, bf16[64,1536]{1,0:T(8,128)(2,1)S(1)}, u32[]{:S(2)}, u32[]{:S(2)}) collective-permute-start(bf16[64,1536]{1,0:T(8,128)(2,1)} %bitcast.10), channel_id=1, source_target_pairs={{0,4},{4,0},{8,12},{12,8},{1,5},{5,1},{9,13},{13,9},{2,6},{6,2},{1... | collective-permute-start | bytes 589832 | tf_op jit(solution)/shard_map/ppermute | solution.py:120
  5.6 0.0 copy-start.1
  5.6 0.7 %copy-done.1 = s32[12,8]{0,1:T(8,128)S(1)} copy-done((s32[12,8]{0,1:T(8,128)S(1)}, s32[12,8]{0,1:T(8,128)}, u32[]{:S(2)}) %copy-start.1) | copy-done | bytes 408
  6.3 2.3 %own.1 = (f32[12,64,128]{2,1,0:T(8,128)S(1)}, s32[3,28]{1,0:T(4,128)S(1)}) custom-call(s32[1]{0:T(128)} %bitcast.3.me_ref, s32[8,12]{1,0:T(8,128)S(1)} %bitcast.8, bf16[64,1536]{1,0:T(8,128)(2,1)} %bitcast.11, bf16[12,8,128,128]{3,2,1,0:T(8,128)(2,1)} %tiles_hbm.3), custom_call_target="tpu_custom_call" | custom-call | flops 25165824 | bytes 1572864 | tf_op jit(solution)/shard_map/own/pallas_call | solution.py:137
  8.6 0.0 copy-start.2
  8.7 0.0 copy-start
  8.7 4.8 %collective-permute-done.two_ref = bf16[64,1536]{1,0:T(8,128)(2,1)S(1)} collective-permute-done((bf16[64,1536]{1,0:T(8,128)(2,1)}, bf16[64,1536]{1,0:T(8,128)(2,1)S(1)}, u32[]{:S(2)}, u32[]{:S(2)}) %collective-permute-start) | collective-permute-done | bytes 196640 | tf_op jit(solution)/shard_map/ppermute | solution.py:120
  13.5 0.7 %collective-permute-start.1 = (bf16[64,1536]{1,0:T(8,128)(2,1)S(1)}, bf16[64,1536]{1,0:T(8,128)(2,1)S(1)}, u32[]{:S(2)}, u32[]{:S(2)}) collective-permute-start(bf16[64,1536]{1,0:T(8,128)(2,1)S(1)} %collective-permute-done.two_ref), channel_id=1, source_target_pairs={{0,4},{4,0},{8,12},{12,8},{1,5},{5,1},{9,13},{13,9},{2,6},{6,2},{1... | collective-permute-start | bytes 589832 | tf_op jit(solution)/shard_map/ppermute | solution.py:120
  14.2 0.0 collective-permute-done.2.one_ref
  14.2 3.5 %middle.1 = (f32[12,64,128]{2,1,0:T(8,128)S(1)}, bf16[28,128,128]{2,1,0:T(8,128)(2,1)S(1)}) custom-call(s32[3,28]{1,0:T(4,128)S(1)} %get-tuple-element.15.list_ref, bf16[64,1536]{1,0:T(8,128)(2,1)S(1)} %collective-permute-done.2.one_ref, bf16[64,1536]{1,0:T(8,128)(2,1)S(1)} %collective-permute-done.two_ref, ...), custom_call_target="tpu_custom_call", output_to_operand_aliasing={{0}: (4, {})} | custom-call | flops 117440512 | bytes 6291456 | tf_op jit(solution)/shard_map/middle/pallas_call | solution.py:156
  17.7 1.8 %collective-permute-done.1.three_ref = bf16[64,1536]{1,0:T(8,128)(2,1)S(1)} collective-permute-done((bf16[64,1536]{1,0:T(8,128)(2,1)S(1)}, bf16[64,1536]{1,0:T(8,128)(2,1)S(1)}, u32[]{:S(2)}, u32[]{:S(2)}) %collective-permute-start.1) | collective-permute-done | bytes 196640 | tf_op jit(solution)/shard_map/ppermute | solution.py:120
  19.5 1.0 %last.1 = (f32[12,64,128]{2,1,0:T(8,128)S(1)}, bf16[64,384]{1,0:T(8,128)(2,1)S(1)}, bf16[64,384]{1,0:T(8,128)(2,1)S(1)}, bf16[64,384]{1,0:T(8,128)(2,1)S(1)}, bf16[64,384]{1,0:T(8,128)(2,1)S(1)}) custom-call(s32[1]{0:T(128)} %bitcast.feat_ref, s32[3,28]{1,0:T(4,128)S(1)} %get-tuple-element.15.list_ref, ...), custom_call_target="tpu_custom_call", output_to_operand_aliasing={{0}: (4, {})} | custom-call | flops 58720256 | bytes 1572864 | tf_op jit(solution)/shard_map/last/pallas_call | solution.py:173
  20.5 0.1 collective-permute-start.3
  20.6 1.3 %collective-permute-start.4 = (bf16[64,384]{1,0:T(8,128)(2,1)S(1)}, bf16[64,384]{1,0:T(8,128)(2,1)S(1)}, u32[]{:S(2)}, u32[]{:S(2)}) collective-permute-start(bf16[64,384]{1,0:T(8,128)(2,1)S(1)} %get-tuple-element.23), channel_id=1, source_target_pairs={{0,2},{1,3},{2,0},{3,1},{4,6},{5,7},{6,4},{7,5},{8,10},{9,11},{10,... | collective-permute-start | bytes 147464 | tf_op jit(solution)/shard_map/ppermute | solution.py:120
  21.9 0.5 %collective-permute-start.5 = (bf16[64,384]{1,0:T(8,128)(2,1)S(1)}, bf16[64,384]{1,0:T(8,128)(2,1)S(1)}, u32[]{:S(2)}, u32[]{:S(2)}) collective-permute-start(bf16[64,384]{1,0:T(8,128)(2,1)S(1)} %get-tuple-element.24), channel_id=1, source_target_pairs={{0,3},{1,2},{2,1},{3,0},{4,7},{5,6},{6,5},{7,4},{8,11},{9,10},{10,... | collective-permute-start | bytes 147464 | tf_op jit(solution)/shard_map/ppermute | solution.py:120
  22.4 0.0 copy-done.2
  22.4 0.1 copy.8.bias_ref
  22.5 0.0 collective-permute-done.3.refs_1_
  22.6 2.2 %collective-permute-done.4.refs_2_ = bf16[64,384]{1,0:T(8,128)(2,1)S(1)} collective-permute-done((bf16[64,384]{1,0:T(8,128)(2,1)S(1)}, bf16[64,384]{1,0:T(8,128)(2,1)S(1)}, u32[]{:S(2)}, u32[]{:S(2)}) %collective-permute-start.4) | collective-permute-done | bytes 49184 | tf_op jit(solution)/shard_map/ppermute | solution.py:120
  24.7 0.9 %collective-permute-done.5.refs_3_ = bf16[64,384]{1,0:T(8,128)(2,1)S(1)} collective-permute-done((bf16[64,384]{1,0:T(8,128)(2,1)S(1)}, bf16[64,384]{1,0:T(8,128)(2,1)S(1)}, u32[]{:S(2)}, u32[]{:S(2)}) %collective-permute-start.5) | collective-permute-done | bytes 49184 | tf_op jit(solution)/shard_map/ppermute | solution.py:120
  25.6 0.0 copy-done
  25.6 0.9 %project.1 = bf16[172,384]{1,0:T(8,128)(2,1)} custom-call(s32[1]{0:T(128)} %bitcast.feat_ref, bf16[172,256]{1,0:T(8,128)(2,1)S(1)} %bitcast.7, f32[172,1]{1,0:T(8,128)S(1)} %copy.8.bias_ref, bf16[64,384]{1,0:T(8,128)(2,1)S(1)} %get-tuple-element.21.refs_0_, bf16[64,384]{1,0:T(8,128)(2,1)S(1)} %collective-permute-done.3.refs_1_, ...), custom_call_target="tpu_custom_call" | custom-call | tf_op jit(solution)/shard_map/project/pallas_call | solution.py:190
Async XLA Ops:
  0.0 13.5 %collective-permute-start = (bf16[64,1536]{1,0:T(8,128)(2,1)}, bf16[64,1536]{1,0:T(8,128)(2,1)S(1)}, u32[]{:S(2)}, u32[]{:S(2)}) collective-permute-start(bf16[64,1536]{1,0:T(8,128)(2,1)} %bitcast.9), channel_id=1, source_target_pairs={{0,8},{4,12},{8,0},{12,4},{1,9},{5,13},{9,1},{13,5},{2,10},{6,14},... | collective-permute-start | bytes 589832 | tf_op jit(solution)/shard_map/ppermute | solution.py:120
  4.0 10.2 %collective-permute-start.2 = (bf16[64,1536]{1,0:T(8,128)(2,1)}, bf16[64,1536]{1,0:T(8,128)(2,1)S(1)}, u32[]{:S(2)}, u32[]{:S(2)}) collective-permute-start(bf16[64,1536]{1,0:T(8,128)(2,1)} %bitcast.10), channel_id=1, source_target_pairs={{0,4},{4,0},{8,12},{12,8},{1,5},{5,1},{9,13},{13,9},{2,6},{6,2},{1... | collective-permute-start | bytes 589832 | tf_op jit(solution)/shard_map/ppermute | solution.py:120
  5.6 0.7 %copy-start.1 = (s32[12,8]{0,1:T(8,128)S(1)}, s32[12,8]{0,1:T(8,128)}, u32[]{:S(2)}) copy-start(s32[12,8]{0,1:T(8,128)} %param.7) | copy-start | bytes 1156
  8.6 13.8 %copy-start.2 = (f32[172]{0:T(256)S(1)}, f32[172]{0:T(256)}, u32[]{:S(2)}) copy-start(f32[172]{0:T(256)} %param.9) | copy-start | bytes 2068
  8.7 16.9 %copy-start = (bf16[256,172]{0,1:T(8,128)(2,1)S(1)}, bf16[256,172]{0,1:T(8,128)(2,1)}, u32[]{:S(2)}) copy-start(bf16[256,172]{0,1:T(8,128)(2,1)} %param.8) | copy-start | bytes 264196
  13.5 6.0 %collective-permute-start.1 = (bf16[64,1536]{1,0:T(8,128)(2,1)S(1)}, bf16[64,1536]{1,0:T(8,128)(2,1)S(1)}, u32[]{:S(2)}, u32[]{:S(2)}) collective-permute-start(bf16[64,1536]{1,0:T(8,128)(2,1)S(1)} %collective-permute-done.two_ref), channel_id=1, source_target_pairs={{0,4},{4,0},{8,12},{12,8},{1,5},{5,1},{9,13},{13,9},{2,6},{6,2},{1... | collective-permute-start | bytes 589832 | tf_op jit(solution)/shard_map/ppermute | solution.py:120
  20.5 2.1 %collective-permute-start.3 = (bf16[64,384]{1,0:T(8,128)(2,1)S(1)}, bf16[64,384]{1,0:T(8,128)(2,1)S(1)}, u32[]{:S(2)}, u32[]{:S(2)}) collective-permute-start(bf16[64,384]{1,0:T(8,128)(2,1)S(1)} %get-tuple-element.22), channel_id=1, source_target_pairs={{0,1},{1,0},{2,3},{3,2},{4,5},{5,4},{6,7},{7,6},{8,9},{9,8},{10,11... | collective-permute-start | bytes 147464 | tf_op jit(solution)/shard_map/ppermute | solution.py:120
  20.6 4.2 %collective-permute-start.4 = (bf16[64,384]{1,0:T(8,128)(2,1)S(1)}, bf16[64,384]{1,0:T(8,128)(2,1)S(1)}, u32[]{:S(2)}, u32[]{:S(2)}) collective-permute-start(bf16[64,384]{1,0:T(8,128)(2,1)S(1)} %get-tuple-element.23), channel_id=1, source_target_pairs={{0,2},{1,3},{2,0},{3,1},{4,6},{5,7},{6,4},{7,5},{8,10},{9,11},{10,... | collective-permute-start | bytes 147464 | tf_op jit(solution)/shard_map/ppermute | solution.py:120
  21.9 3.7 %collective-permute-start.5 = (bf16[64,384]{1,0:T(8,128)(2,1)S(1)}, bf16[64,384]{1,0:T(8,128)(2,1)S(1)}, u32[]{:S(2)}, u32[]{:S(2)}) collective-permute-start(bf16[64,384]{1,0:T(8,128)(2,1)S(1)} %get-tuple-element.24), channel_id=1, source_target_pairs={{0,3},{1,2},{2,1},{3,0},{4,7},{5,6},{6,5},{7,4},{8,11},{9,10},{10,... | collective-permute-start | bytes 147464 | tf_op jit(solution)/shard_map/ppermute | solution.py:120

commit v4 on v3

--- a/solution.py
+++ b/solution.py
@@ -156,7 +156,7 @@
     acc, three_tiles = pl.pallas_call(
         middle_kernel,
         out_shape=(acc_shape, held),
-        in_specs=[SMEM, VMEM, VMEM, HBM, VMEM],
+        in_specs=[VMEM, VMEM, VMEM, HBM, VMEM],
         out_specs=(VMEM, VMEM),
         input_output_aliases={4: 0},
         scratch_shapes=[
@@ -168,12 +168,12 @@
             flops=2 * remote * tile_flops, bytes_accessed=tiles.size * 4, transcendentals=0
         ),
         name="middle",
-    )(lists, *in_vmem(one, ready), in_hbm(tiles), *in_vmem(acc))
+    )(*in_vmem(lists, one, ready), in_hbm(tiles), *in_vmem(acc))
     part_shape = pltpu.VMEM((width, stripe_blocks // slices * size), jnp.bfloat16)
     _, *parts = pl.pallas_call(
         functools.partial(last_kernel, slot_count),
         out_shape=(acc_shape,) + (part_shape,) * slices,
-        in_specs=[SMEM, SMEM, VMEM, VMEM, VMEM],
+        in_specs=[SMEM, VMEM, VMEM, VMEM, VMEM],
         out_specs=(VMEM,) * (1 + slices),
         input_output_aliases={4: 0},
         compiler_params=params,
@@ -181,7 +181,7 @@
             flops=remote * tile_flops, bytes_accessed=tiles.size, transcendentals=0
         ),
         name="last",
-    )(feat, lists, *in_vmem(three, three_tiles, acc))
+    )(feat, *in_vmem(lists, three, three_tiles, acc))
     parts = parts[:1] + [
         exchange(parts[k], "feat", slices, k) for k in range(1, slices)
     ]

time: 26.7 us -> 26.2 us (0.981)
  Pallas kernels: 7.71 us -> 6.94 us
  waiting for transfers between devices: 9.62 us -> 9.92 us
    pallas_call x1, Pallas kernels: 0.98 us -> 0.51 us  [on_line(): pl.pallas_call(functools.partial(last_kernel, slot_count), out_shape=(acc...]
    pallas_call x1, Pallas kernels: 3.51 us -> 3.21 us  [on_line(): pl.pallas_call(middle_kernel, out_shape=(acc_shape, held), in_specs=[VMEM...]
    ppermute x6, waiting for transfers between devices: 9.62 us -> 9.92 us  [exchange(): return lax.ppermute(x, axis, [(i, i ^ bit) for i in range(size)])]
  transfers between devices with their start and end apart: 6 -> 6, of which waited for: 4 -> 4; matrix products, arithmetic and copies ran while one was open for 0% -> 0% of each run, Pallas kernels for 22% -> 21%
where the time goes in v4:
time: 26.2 us; the launch traced here: 26 us
  waiting for transfers between devices  9.92 us (38%)
  starting transfers between devices  8.27 us (32%)
  Pallas kernels  6.94 us (26%)
  local copies, waits for them, and re-layouts  0.81 us (3%)
    ppermute x6, waiting for transfers between devices, exchange(): return lax.ppermute(x, axis, [(i, i ^ bit) for i in range(size)])  9.92 us
    ppermute x6, starting transfers between devices, exchange(): return lax.ppermute(x, axis, [(i, i ^ bit) for i in range(size)])  8.27 us
    pallas_call x1, Pallas kernels, on_line(): pl.pallas_call(middle_kernel, out_shape=(acc_shape, held), in_specs=[VMEM...  3.21 us
    pallas_call x1, Pallas kernels, on_line(): pl.pallas_call(own_kernel, out_shape=(acc_shape, jax.ShapeDtypeStruct((st...  2.34 us
    pallas_call x1, Pallas kernels, on_line(): pl.pallas_call(project_kernel, out_shape=jax.ShapeDtypeStruct((classes, r...  0.88 us
    unnamed x6, local copies, waits for them, and re-layouts  0.7 us
  transfers between devices with their start and end apart: 6, of which 4 were waited for; matrix products, arithmetic and copies ran while one was open for 0% of the time, Pallas kernels for 21%

profile of v4, /device:TPU:0, one launch (start us, length us, event | category | flops | bytes accessed | tf_op | source)
XLA Modules:
  0.0 26.0 jit_solution(5270244827342242815)
XLA Ops:
  0.0 4.0 %collective-permute-start = (bf16[64,1536]{1,0:T(8,128)(2,1)}, bf16[64,1536]{1,0:T(8,128)(2,1)S(1)}, u32[]{:S(2)}, u32[]{:S(2)}) collective-permute-start(bf16[64,1536]{1,0:T(8,128)(2,1)} %bitcast.9), channel_id=1, source_target_pairs={{0,8},{4,12},{8,0},{12,4},{1,9},{5,13},{9,1},{13,5},{2,10},{6,14},... | collective-permute-start | bytes 589832 | tf_op jit(solution)/shard_map/ppermute | solution.py:120
  4.0 1.6 %collective-permute-start.2 = (bf16[64,1536]{1,0:T(8,128)(2,1)}, bf16[64,1536]{1,0:T(8,128)(2,1)S(1)}, u32[]{:S(2)}, u32[]{:S(2)}) collective-permute-start(bf16[64,1536]{1,0:T(8,128)(2,1)} %bitcast.10), channel_id=1, source_target_pairs={{0,4},{4,0},{8,12},{12,8},{1,5},{5,1},{9,13},{13,9},{2,6},{6,2},{1... | collective-permute-start | bytes 589832 | tf_op jit(solution)/shard_map/ppermute | solution.py:120
  5.6 0.0 copy-start.1
  5.6 0.7 %copy-done.1 = s32[12,8]{0,1:T(8,128)S(1)} copy-done((s32[12,8]{0,1:T(8,128)S(1)}, s32[12,8]{0,1:T(8,128)}, u32[]{:S(2)}) %copy-start.1) | copy-done | bytes 408
  6.3 2.3 %own.1 = (f32[12,64,128]{2,1,0:T(8,128)S(1)}, s32[3,28]{1,0:T(4,128)S(1)}) custom-call(s32[1]{0:T(128)} %bitcast.3.me_ref, s32[8,12]{1,0:T(8,128)S(1)} %bitcast.8, bf16[64,1536]{1,0:T(8,128)(2,1)} %bitcast.11, bf16[12,8,128,128]{3,2,1,0:T(8,128)(2,1)} %tiles_hbm.3), custom_call_target="tpu_custom_call" | custom-call | flops 25165824 | bytes 1572864 | tf_op jit(solution)/shard_map/own/pallas_call | solution.py:137
  8.6 0.0 copy-start.2
  8.7 0.0 copy-start
  8.7 4.8 %collective-permute-done.two_ref = bf16[64,1536]{1,0:T(8,128)(2,1)S(1)} collective-permute-done((bf16[64,1536]{1,0:T(8,128)(2,1)}, bf16[64,1536]{1,0:T(8,128)(2,1)S(1)}, u32[]{:S(2)}, u32[]{:S(2)}) %collective-permute-start) | collective-permute-done | bytes 196640 | tf_op jit(solution)/shard_map/ppermute | solution.py:120
  13.5 0.7 %collective-permute-start.1 = (bf16[64,1536]{1,0:T(8,128)(2,1)S(1)}, bf16[64,1536]{1,0:T(8,128)(2,1)S(1)}, u32[]{:S(2)}, u32[]{:S(2)}) collective-permute-start(bf16[64,1536]{1,0:T(8,128)(2,1)S(1)} %collective-permute-done.two_ref), channel_id=1, source_target_pairs={{0,4},{4,0},{8,12},{12,8},{1,5},{5,1},{9,13},{13,9},{2,6},{6,2},{1... | collective-permute-start | bytes 589832 | tf_op jit(solution)/shard_map/ppermute | solution.py:120
  14.2 0.0 collective-permute-done.2.one_ref
  14.2 3.2 %middle.1 = (f32[12,64,128]{2,1,0:T(8,128)S(1)}, bf16[28,128,128]{2,1,0:T(8,128)(2,1)S(1)}) custom-call(s32[3,28]{1,0:T(4,128)S(1)} %get-tuple-element.15.list_ref, bf16[64,1536]{1,0:T(8,128)(2,1)S(1)} %collective-permute-done.2.one_ref, bf16[64,1536]{1,0:T(8,128)(2,1)S(1)} %collective-permute-done.two_ref, ...), custom_call_target="tpu_custom_call", output_to_operand_aliasing={{0}: (4, {})} | custom-call | flops 117440512 | bytes 6291456 | tf_op jit(solution)/shard_map/middle/pallas_call | solution.py:156
  17.4 2.1 %collective-permute-done.1.three_ref = bf16[64,1536]{1,0:T(8,128)(2,1)S(1)} collective-permute-done((bf16[64,1536]{1,0:T(8,128)(2,1)S(1)}, bf16[64,1536]{1,0:T(8,128)(2,1)S(1)}, u32[]{:S(2)}, u32[]{:S(2)}) %collective-permute-start.1) | collective-permute-done | bytes 196640 | tf_op jit(solution)/shard_map/ppermute | solution.py:120
  19.5 0.5 %last.1 = (f32[12,64,128]{2,1,0:T(8,128)S(1)}, bf16[64,384]{1,0:T(8,128)(2,1)S(1)}, bf16[64,384]{1,0:T(8,128)(2,1)S(1)}, bf16[64,384]{1,0:T(8,128)(2,1)S(1)}, bf16[64,384]{1,0:T(8,128)(2,1)S(1)}) custom-call(s32[1]{0:T(128)} %bitcast.feat_ref, s32[3,28]{1,0:T(4,128)S(1)} %get-tuple-element.15.list_ref, ...), custom_call_target="tpu_custom_call", output_to_operand_aliasing={{0}: (4, {})} | custom-call | flops 58720256 | bytes 1572864 | tf_op jit(solution)/shard_map/last/pallas_call | solution.py:173
  20.0 0.1 collective-permute-start.3
  20.1 1.3 %collective-permute-start.4 = (bf16[64,384]{1,0:T(8,128)(2,1)S(1)}, bf16[64,384]{1,0:T(8,128)(2,1)S(1)}, u32[]{:S(2)}, u32[]{:S(2)}) collective-permute-start(bf16[64,384]{1,0:T(8,128)(2,1)S(1)} %get-tuple-element.23), channel_id=1, source_target_pairs={{0,2},{1,3},{2,0},{3,1},{4,6},{5,7},{6,4},{7,5},{8,10},{9,11},{10,... | collective-permute-start | bytes 147464 | tf_op jit(solution)/shard_map/ppermute | solution.py:120
  21.4 0.5 %collective-permute-start.5 = (bf16[64,384]{1,0:T(8,128)(2,1)S(1)}, bf16[64,384]{1,0:T(8,128)(2,1)S(1)}, u32[]{:S(2)}, u32[]{:S(2)}) collective-permute-start(bf16[64,384]{1,0:T(8,128)(2,1)S(1)} %get-tuple-element.24), channel_id=1, source_target_pairs={{0,3},{1,2},{2,1},{3,0},{4,7},{5,6},{6,5},{7,4},{8,11},{9,10},{10,... | collective-permute-start | bytes 147464 | tf_op jit(solution)/shard_map/ppermute | solution.py:120
  21.9 0.0 copy-done.2
  22.0 0.1 copy.8.bias_ref
  22.1 0.0 collective-permute-done.3.refs_1_
  22.1 2.2 %collective-permute-done.4.refs_2_ = bf16[64,384]{1,0:T(8,128)(2,1)S(1)} collective-permute-done((bf16[64,384]{1,0:T(8,128)(2,1)S(1)}, bf16[64,384]{1,0:T(8,128)(2,1)S(1)}, u32[]{:S(2)}, u32[]{:S(2)}) %collective-permute-start.4) | collective-permute-done | bytes 49184 | tf_op jit(solution)/shard_map/ppermute | solution.py:120
  24.2 0.9 %collective-permute-done.5.refs_3_ = bf16[64,384]{1,0:T(8,128)(2,1)S(1)} collective-permute-done((bf16[64,384]{1,0:T(8,128)(2,1)S(1)}, bf16[64,384]{1,0:T(8,128)(2,1)S(1)}, u32[]{:S(2)}, u32[]{:S(2)}) %collective-permute-start.5) | collective-permute-done | bytes 49184 | tf_op jit(solution)/shard_map/ppermute | solution.py:120
  25.1 0.0 copy-done
  25.1 0.9 %project.1 = bf16[172,384]{1,0:T(8,128)(2,1)} custom-call(s32[1]{0:T(128)} %bitcast.feat_ref, bf16[172,256]{1,0:T(8,128)(2,1)S(1)} %bitcast.7, f32[172,1]{1,0:T(8,128)S(1)} %copy.8.bias_ref, bf16[64,384]{1,0:T(8,128)(2,1)S(1)} %get-tuple-element.21.refs_0_, bf16[64,384]{1,0:T(8,128)(2,1)S(1)} %collective-permute-done.3.refs_1_, ...), custom_call_target="tpu_custom_call" | custom-call | tf_op jit(solution)/shard_map/project/pallas_call | solution.py:190
Async XLA Ops:
  0.0 13.5 %collective-permute-start = (bf16[64,1536]{1,0:T(8,128)(2,1)}, bf16[64,1536]{1,0:T(8,128)(2,1)S(1)}, u32[]{:S(2)}, u32[]{:S(2)}) collective-permute-start(bf16[64,1536]{1,0:T(8,128)(2,1)} %bitcast.9), channel_id=1, source_target_pairs={{0,8},{4,12},{8,0},{12,4},{1,9},{5,13},{9,1},{13,5},{2,10},{6,14},... | collective-permute-start | bytes 589832 | tf_op jit(solution)/shard_map/ppermute | solution.py:120
  4.0 10.2 %collective-permute-start.2 = (bf16[64,1536]{1,0:T(8,128)(2,1)}, bf16[64,1536]{1,0:T(8,128)(2,1)S(1)}, u32[]{:S(2)}, u32[]{:S(2)}) collective-permute-start(bf16[64,1536]{1,0:T(8,128)(2,1)} %bitcast.10), channel_id=1, source_target_pairs={{0,4},{4,0},{8,12},{12,8},{1,5},{5,1},{9,13},{13,9},{2,6},{6,2},{1... | collective-permute-start | bytes 589832 | tf_op jit(solution)/shard_map/ppermute | solution.py:120
  5.6 0.7 %copy-start.1 = (s32[12,8]{0,1:T(8,128)S(1)}, s32[12,8]{0,1:T(8,128)}, u32[]{:S(2)}) copy-start(s32[12,8]{0,1:T(8,128)} %param.7) | copy-start | bytes 1156
  8.6 13.3 %copy-start.2 = (f32[172]{0:T(256)S(1)}, f32[172]{0:T(256)}, u32[]{:S(2)}) copy-start(f32[172]{0:T(256)} %param.9) | copy-start | bytes 2068
  8.7 16.5 %copy-start = (bf16[256,172]{0,1:T(8,128)(2,1)S(1)}, bf16[256,172]{0,1:T(8,128)(2,1)}, u32[]{:S(2)}) copy-start(bf16[256,172]{0,1:T(8,128)(2,1)} %param.8) | copy-start | bytes 264196
  13.5 6.0 %collective-permute-start.1 = (bf16[64,1536]{1,0:T(8,128)(2,1)S(1)}, bf16[64,1536]{1,0:T(8,128)(2,1)S(1)}, u32[]{:S(2)}, u32[]{:S(2)}) collective-permute-start(bf16[64,1536]{1,0:T(8,128)(2,1)S(1)} %collective-permute-done.two_ref), channel_id=1, source_target_pairs={{0,4},{4,0},{8,12},{12,8},{1,5},{5,1},{9,13},{13,9},{2,6},{6,2},{1... | collective-permute-start | bytes 589832 | tf_op jit(solution)/shard_map/ppermute | solution.py:120
  20.0 2.1 %collective-permute-start.3 = (bf16[64,384]{1,0:T(8,128)(2,1)S(1)}, bf16[64,384]{1,0:T(8,128)(2,1)S(1)}, u32[]{:S(2)}, u32[]{:S(2)}) collective-permute-start(bf16[64,384]{1,0:T(8,128)(2,1)S(1)} %get-tuple-element.22), channel_id=1, source_target_pairs={{0,1},{1,0},{2,3},{3,2},{4,5},{5,4},{6,7},{7,6},{8,9},{9,8},{10,11... | collective-permute-start | bytes 147464 | tf_op jit(solution)/shard_map/ppermute | solution.py:120
  20.1 4.2 %collective-permute-start.4 = (bf16[64,384]{1,0:T(8,128)(2,1)S(1)}, bf16[64,384]{1,0:T(8,128)(2,1)S(1)}, u32[]{:S(2)}, u32[]{:S(2)}) collective-permute-start(bf16[64,384]{1,0:T(8,128)(2,1)S(1)} %get-tuple-element.23), channel_id=1, source_target_pairs={{0,2},{1,3},{2,0},{3,1},{4,6},{5,7},{6,4},{7,5},{8,10},{9,11},{10,... | collective-permute-start | bytes 147464 | tf_op jit(solution)/shard_map/ppermute | solution.py:120
  21.4 3.7 %collective-permute-start.5 = (bf16[64,384]{1,0:T(8,128)(2,1)S(1)}, bf16[64,384]{1,0:T(8,128)(2,1)S(1)}, u32[]{:S(2)}, u32[]{:S(2)}) collective-permute-start(bf16[64,384]{1,0:T(8,128)(2,1)S(1)} %get-tuple-element.24), channel_id=1, source_target_pairs={{0,3},{1,2},{2,1},{3,0},{4,7},{5,6},{6,5},{7,4},{8,11},{9,10},{10,... | collective-permute-start | bytes 147464 | tf_op jit(solution)/shard_map/ppermute | solution.py:120

commit v5 on v4

--- a/solution.py
+++ b/solution.py
@@ -90,7 +90,7 @@
     add_slots(2, list_ref, three_ref, tiles_ref, acc_ref, slot_count, times_turned)
     size = tiles_ref.shape[-1]
     share = acc_ref.shape[0] // len(part_refs)
-    for k, part_ref in enumerate(part_refs):
+    for k, part_ref in enumerate(reversed(part_refs)):
         owner = feat_ref[0] ^ k
         for row in range(share):
             part_ref[:, row * size : (row + 1) * size] = acc_ref[
@@ -101,7 +101,7 @@
 def project_kernel(feat_ref, weight_ref, bias_ref, *refs):
     part_refs, out_ref, rows = refs[:-2], refs[-2], refs[-1]
     width = part_refs[0].shape[0]
-    for k, part_ref in enumerate(part_refs):
+    for k, part_ref in enumerate(reversed(part_refs)):
         owner = feat_ref[0] ^ k
         rows[pl.ds(pl.multiple_of(owner * width, width), width), :] = part_ref[...]
     total = jnp.dot(weight_ref[...], rows[...], preferred_element_type=jnp.float32)
@@ -182,8 +182,9 @@
         ),
         name="last",
     )(feat, *in_vmem(lists, three, three_tiles, acc))
-    parts = parts[:1] + [
-        exchange(parts[k], "feat", slices, k) for k in range(1, slices)
+    parts = [
+        exchange(part, "feat", slices, slices - 1 - k) if k < slices - 1 else part
+        for k, part in enumerate(parts)
     ]
     rows = part_shape.shape[1]
     classes = weight.shape[1]

time: 26.2 us -> 25.9 us (0.989)
  waiting for transfers between devices: 9.92 us -> 9.63 us
    ppermute x6, waiting for transfers between devices: 9.92 us -> 9.63 us  [exchange(): return lax.ppermute(x, axis, [(i, i ^ bit) for i in range(size)])]
  transfers between devices with their start and end apart: 6 -> 6, of which waited for: 4 -> 4; matrix products, arithmetic and copies ran while one was open for 0% -> 0% of each run, Pallas kernels for 21% -> 22%
where the time goes in v5:
time: 25.9 us; the launch traced here: 25.7 us
  waiting for transfers between devices  9.63 us (37%)
  starting transfers between devices  8.25 us (32%)
  Pallas kernels  6.94 us (27%)
  local copies, waits for them, and re-layouts  0.81 us (3%)
    ppermute x6, waiting for transfers between devices, exchange(): return lax.ppermute(x, axis, [(i, i ^ bit) for i in range(size)])  9.63 us
    ppermute x6, starting transfers between devices, exchange(): return lax.ppermute(x, axis, [(i, i ^ bit) for i in range(size)])  8.25 us
    pallas_call x1, Pallas kernels, on_line(): pl.pallas_call(middle_kernel, out_shape=(acc_shape, held), in_specs=[VMEM...  3.21 us
    pallas_call x1, Pallas kernels, on_line(): pl.pallas_call(own_kernel, out_shape=(acc_shape, jax.ShapeDtypeStruct((st...  2.34 us
    pallas_call x1, Pallas kernels, on_line(): pl.pallas_call(project_kernel, out_shape=jax.ShapeDtypeStruct((classes, r...  0.88 us
    unnamed x6, local copies, waits for them, and re-layouts  0.7 us
  transfers between devices with their start and end apart: 6, of which 4 were waited for; matrix products, arithmetic and copies ran while one was open for 0% of the time, Pallas kernels for 22%

profile of v5, /device:TPU:0, one launch (start us, length us, event | category | flops | bytes accessed | tf_op | source)
XLA Modules:
  0.0 25.7 jit_solution(6814101677665263671)
XLA Ops:
  0.0 4.0 %collective-permute-start = (bf16[64,1536]{1,0:T(8,128)(2,1)}, bf16[64,1536]{1,0:T(8,128)(2,1)S(1)}, u32[]{:S(2)}, u32[]{:S(2)}) collective-permute-start(bf16[64,1536]{1,0:T(8,128)(2,1)} %bitcast.9), channel_id=1, source_target_pairs={{0,8},{4,12},{8,0},{12,4},{1,9},{5,13},{9,1},{13,5},{2,10},{6,14},... | collective-permute-start | bytes 589832 | tf_op jit(solution)/shard_map/ppermute | solution.py:120
  4.0 1.6 %collective-permute-start.2 = (bf16[64,1536]{1,0:T(8,128)(2,1)}, bf16[64,1536]{1,0:T(8,128)(2,1)S(1)}, u32[]{:S(2)}, u32[]{:S(2)}) collective-permute-start(bf16[64,1536]{1,0:T(8,128)(2,1)} %bitcast.10), channel_id=1, source_target_pairs={{0,4},{4,0},{8,12},{12,8},{1,5},{5,1},{9,13},{13,9},{2,6},{6,2},{1... | collective-permute-start | bytes 589832 | tf_op jit(solution)/shard_map/ppermute | solution.py:120
  5.6 0.0 copy-start.1
  5.6 0.7 %copy-done.1 = s32[12,8]{0,1:T(8,128)S(1)} copy-done((s32[12,8]{0,1:T(8,128)S(1)}, s32[12,8]{0,1:T(8,128)}, u32[]{:S(2)}) %copy-start.1) | copy-done | bytes 408
  6.3 2.3 %own.1 = (f32[12,64,128]{2,1,0:T(8,128)S(1)}, s32[3,28]{1,0:T(4,128)S(1)}) custom-call(s32[1]{0:T(128)} %bitcast.3.me_ref, s32[8,12]{1,0:T(8,128)S(1)} %bitcast.8, bf16[64,1536]{1,0:T(8,128)(2,1)} %bitcast.11, bf16[12,8,128,128]{3,2,1,0:T(8,128)(2,1)} %tiles_hbm.3), custom_call_target="tpu_custom_call" | custom-call | flops 25165824 | bytes 1572864 | tf_op jit(solution)/shard_map/own/pallas_call | solution.py:137
  8.6 0.0 copy-start.2
  8.7 0.0 copy-start
  8.7 4.8 %collective-permute-done.two_ref = bf16[64,1536]{1,0:T(8,128)(2,1)S(1)} collective-permute-done((bf16[64,1536]{1,0:T(8,128)(2,1)}, bf16[64,1536]{1,0:T(8,128)(2,1)S(1)}, u32[]{:S(2)}, u32[]{:S(2)}) %collective-permute-start) | collective-permute-done | bytes 196640 | tf_op jit(solution)/shard_map/ppermute | solution.py:120
  13.5 0.7 %collective-permute-start.1 = (bf16[64,1536]{1,0:T(8,128)(2,1)S(1)}, bf16[64,1536]{1,0:T(8,128)(2,1)S(1)}, u32[]{:S(2)}, u32[]{:S(2)}) collective-permute-start(bf16[64,1536]{1,0:T(8,128)(2,1)S(1)} %collective-permute-done.two_ref), channel_id=1, source_target_pairs={{0,4},{4,0},{8,12},{12,8},{1,5},{5,1},{9,13},{13,9},{2,6},{6,2},{1... | collective-permute-start | bytes 589832 | tf_op jit(solution)/shard_map/ppermute | solution.py:120
  14.2 0.0 collective-permute-done.2.one_ref
  14.2 3.2 %middle.1 = (f32[12,64,128]{2,1,0:T(8,128)S(1)}, bf16[28,128,128]{2,1,0:T(8,128)(2,1)S(1)}) custom-call(s32[3,28]{1,0:T(4,128)S(1)} %get-tuple-element.15.list_ref, bf16[64,1536]{1,0:T(8,128)(2,1)S(1)} %collective-permute-done.2.one_ref, bf16[64,1536]{1,0:T(8,128)(2,1)S(1)} %collective-permute-done.two_ref, ...), custom_call_target="tpu_custom_call", output_to_operand_aliasing={{0}: (4, {})} | custom-call | flops 117440512 | bytes 6291456 | tf_op jit(solution)/shard_map/middle/pallas_call | solution.py:156
  17.4 2.1 %collective-permute-done.1.three_ref = bf16[64,1536]{1,0:T(8,128)(2,1)S(1)} collective-permute-done((bf16[64,1536]{1,0:T(8,128)(2,1)S(1)}, bf16[64,1536]{1,0:T(8,128)(2,1)S(1)}, u32[]{:S(2)}, u32[]{:S(2)}) %collective-permute-start.1) | collective-permute-done | bytes 196640 | tf_op jit(solution)/shard_map/ppermute | solution.py:120
  19.5 0.5 %last.1 = (f32[12,64,128]{2,1,0:T(8,128)S(1)}, bf16[64,384]{1,0:T(8,128)(2,1)S(1)}, bf16[64,384]{1,0:T(8,128)(2,1)S(1)}, bf16[64,384]{1,0:T(8,128)(2,1)S(1)}, bf16[64,384]{1,0:T(8,128)(2,1)S(1)}) custom-call(s32[1]{0:T(128)} %bitcast.feat_ref, s32[3,28]{1,0:T(4,128)S(1)} %get-tuple-element.15.list_ref, ...), custom_call_target="tpu_custom_call", output_to_operand_aliasing={{0}: (4, {})} | custom-call | flops 58720256 | bytes 1572864 | tf_op jit(solution)/shard_map/last/pallas_call | solution.py:173
  20.0 0.1 collective-permute-start.3
  20.1 1.3 %collective-permute-start.4 = (bf16[64,384]{1,0:T(8,128)(2,1)S(1)}, bf16[64,384]{1,0:T(8,128)(2,1)S(1)}, u32[]{:S(2)}, u32[]{:S(2)}) collective-permute-start(bf16[64,384]{1,0:T(8,128)(2,1)S(1)} %get-tuple-element.22), channel_id=1, source_target_pairs={{0,2},{1,3},{2,0},{3,1},{4,6},{5,7},{6,4},{7,5},{8,10},{9,11},{10,... | collective-permute-start | bytes 147464 | tf_op jit(solution)/shard_map/ppermute | solution.py:120
  21.4 0.5 %collective-permute-start.5 = (bf16[64,384]{1,0:T(8,128)(2,1)S(1)}, bf16[64,384]{1,0:T(8,128)(2,1)S(1)}, u32[]{:S(2)}, u32[]{:S(2)}) collective-permute-start(bf16[64,384]{1,0:T(8,128)(2,1)S(1)} %get-tuple-element.23), channel_id=1, source_target_pairs={{0,1},{1,0},{2,3},{3,2},{4,5},{5,4},{6,7},{7,6},{8,9},{9,8},{10,11... | collective-permute-start | bytes 147464 | tf_op jit(solution)/shard_map/ppermute | solution.py:120
  21.9 0.0 copy-done.2
  21.9 0.1 copy.8.bias_ref
  22.1 2.1 %collective-permute-done.3.refs_0_ = bf16[64,384]{1,0:T(8,128)(2,1)S(1)} collective-permute-done((bf16[64,384]{1,0:T(8,128)(2,1)S(1)}, bf16[64,384]{1,0:T(8,128)(2,1)S(1)}, u32[]{:S(2)}, u32[]{:S(2)}) %collective-permute-start.3) | collective-permute-done | bytes 49184 | tf_op jit(solution)/shard_map/ppermute | solution.py:120
  24.1 0.7 %collective-permute-done.4.refs_1_ = bf16[64,384]{1,0:T(8,128)(2,1)S(1)} collective-permute-done((bf16[64,384]{1,0:T(8,128)(2,1)S(1)}, bf16[64,384]{1,0:T(8,128)(2,1)S(1)}, u32[]{:S(2)}, u32[]{:S(2)}) %collective-permute-start.4) | collective-permute-done | bytes 49184 | tf_op jit(solution)/shard_map/ppermute | solution.py:120
  24.8 0.0 collective-permute-done.5.refs_2_
  24.8 0.0 copy-done
  24.8 0.9 %project.1 = bf16[172,384]{1,0:T(8,128)(2,1)} custom-call(s32[1]{0:T(128)} %bitcast.feat_ref, bf16[172,256]{1,0:T(8,128)(2,1)S(1)} %bitcast.7, f32[172,1]{1,0:T(8,128)S(1)} %copy.8.bias_ref, bf16[64,384]{1,0:T(8,128)(2,1)S(1)} %collective-permute-done.3.refs_0_, bf16[64,384]{1,0:T(8,128)(2,1)S(1)} %collective-permute-done.4.refs_1_, ...), custom_call_target="tpu_custom_call" | custom-call | tf_op jit(solution)/shard_map/project/pallas_call | solution.py:191
Async XLA Ops:
  0.0 13.5 %collective-permute-start = (bf16[64,1536]{1,0:T(8,128)(2,1)}, bf16[64,1536]{1,0:T(8,128)(2,1)S(1)}, u32[]{:S(2)}, u32[]{:S(2)}) collective-permute-start(bf16[64,1536]{1,0:T(8,128)(2,1)} %bitcast.9), channel_id=1, source_target_pairs={{0,8},{4,12},{8,0},{12,4},{1,9},{5,13},{9,1},{13,5},{2,10},{6,14},... | collective-permute-start | bytes 589832 | tf_op jit(solution)/shard_map/ppermute | solution.py:120
  4.0 10.2 %collective-permute-start.2 = (bf16[64,1536]{1,0:T(8,128)(2,1)}, bf16[64,1536]{1,0:T(8,128)(2,1)S(1)}, u32[]{:S(2)}, u32[]{:S(2)}) collective-permute-start(bf16[64,1536]{1,0:T(8,128)(2,1)} %bitcast.10), channel_id=1, source_target_pairs={{0,4},{4,0},{8,12},{12,8},{1,5},{5,1},{9,13},{13,9},{2,6},{6,2},{1... | collective-permute-start | bytes 589832 | tf_op jit(solution)/shard_map/ppermute | solution.py:120
  5.6 0.7 %copy-start.1 = (s32[12,8]{0,1:T(8,128)S(1)}, s32[12,8]{0,1:T(8,128)}, u32[]{:S(2)}) copy-start(s32[12,8]{0,1:T(8,128)} %param.7) | copy-start | bytes 1156
  8.6 13.3 %copy-start.2 = (f32[172]{0:T(256)S(1)}, f32[172]{0:T(256)}, u32[]{:S(2)}) copy-start(f32[172]{0:T(256)} %param.9) | copy-start | bytes 2068
  8.7 16.2 %copy-start = (bf16[256,172]{0,1:T(8,128)(2,1)S(1)}, bf16[256,172]{0,1:T(8,128)(2,1)}, u32[]{:S(2)}) copy-start(bf16[256,172]{0,1:T(8,128)(2,1)} %param.8) | copy-start | bytes 264196
  13.5 6.0 %collective-permute-start.1 = (bf16[64,1536]{1,0:T(8,128)(2,1)S(1)}, bf16[64,1536]{1,0:T(8,128)(2,1)S(1)}, u32[]{:S(2)}, u32[]{:S(2)}) collective-permute-start(bf16[64,1536]{1,0:T(8,128)(2,1)S(1)} %collective-permute-done.two_ref), channel_id=1, source_target_pairs={{0,4},{4,0},{8,12},{12,8},{1,5},{5,1},{9,13},{13,9},{2,6},{6,2},{1... | collective-permute-start | bytes 589832 | tf_op jit(solution)/shard_map/ppermute | solution.py:120
  20.0 4.1 %collective-permute-start.3 = (bf16[64,384]{1,0:T(8,128)(2,1)S(1)}, bf16[64,384]{1,0:T(8,128)(2,1)S(1)}, u32[]{:S(2)}, u32[]{:S(2)}) collective-permute-start(bf16[64,384]{1,0:T(8,128)(2,1)S(1)} %get-tuple-element.21), channel_id=1, source_target_pairs={{0,3},{1,2},{2,1},{3,0},{4,7},{5,6},{6,5},{7,4},{8,11},{9,10},{10,... | collective-permute-start | bytes 147464 | tf_op jit(solution)/shard_map/ppermute | solution.py:120
  20.1 4.7 %collective-permute-start.4 = (bf16[64,384]{1,0:T(8,128)(2,1)S(1)}, bf16[64,384]{1,0:T(8,128)(2,1)S(1)}, u32[]{:S(2)}, u32[]{:S(2)}) collective-permute-start(bf16[64,384]{1,0:T(8,128)(2,1)S(1)} %get-tuple-element.22), channel_id=1, source_target_pairs={{0,2},{1,3},{2,0},{3,1},{4,6},{5,7},{6,4},{7,5},{8,10},{9,11},{10,... | collective-permute-start | bytes 147464 | tf_op jit(solution)/shard_map/ppermute | solution.py:120
  21.4 3.4 %collective-permute-start.5 = (bf16[64,384]{1,0:T(8,128)(2,1)S(1)}, bf16[64,384]{1,0:T(8,128)(2,1)S(1)}, u32[]{:S(2)}, u32[]{:S(2)}) collective-permute-start(bf16[64,384]{1,0:T(8,128)(2,1)S(1)} %get-tuple-element.23), channel_id=1, source_target_pairs={{0,1},{1,0},{2,3},{3,2},{4,5},{5,4},{6,7},{7,6},{8,9},{9,8},{10,11... | collective-permute-start | bytes 147464 | tf_op jit(solution)/shard_map/ppermute | solution.py:120
